TPU v7x, 256 devices: a whole 4x4x8 slice. The times are simulated.
256 devices in a mesh: dp: 16 (over y, x), expert: 16 (over z, core).
Axes of the slice: x: 4, y: 4, z: 8, core: 2. Of those that a mesh axis runs over, the one named last changes fastest.
Arguments:
- queries: bfloat16 [65536, 4096], P(('dp', 'expert')), may hold values from -6 to 6
- key_rows: bfloat16 [65536, 4096], P(('dp', 'expert')), may hold values from -6 to 6
- value_rows: bfloat16 [65536, 4096], P(('dp', 'expert')), may hold values from -6 to 6
- slopes: float32 [32], replicated, may hold values from 0.002 to 0.1
- norm_gain: float32 [4096], replicated, may hold values from 0.5 to 1.5
- parents: int32 [256], P('dp'), may hold values from 0 to 31
- lengths: int32 [256], P('dp'), may hold values from 1 to 256, 32768 in all
- parent_states: float32 [32, 32, 128, 128], P('dp', 'expert'), may hold values from -96 to 96
Outputs:
- mixed: bfloat16 [65536, 4096], P(('dp', 'expert'))
- child_states: float32 [256, 32, 128, 128], P('dp', 'expert')
Inputs may be any that keep to these rules, and one draw needn't show every extreme that they name: `parents`: index of the parent whose state the child continues. `lengths`: slots past a child's length are padding.
All inputs are finite; a program needn't handle non-finite values. No bound on the sum of `lengths` on one device may be relied on, other than what follows from the above.
Results may differ from a plain program's by a relative error of at most 0.0065.
Values may be sent and summed in bfloat16 or wider, within the bound.
A program may use at most 128 MiB of HBM per device.

v0:
```python
import jax
import jax.numpy as jnp
from jax import lax
from jax.sharding import PartitionSpec as P

EPS = 1e-06
HIGHEST = lax.Precision.HIGHEST


def lightning(query, key_part, value_part, start, lens, slopes):
    length_seg = query.shape[1]
    places = jnp.arange(length_seg, dtype=jnp.float32)
    offset = places[:, None] - places[None, :]
    decays = jnp.where(
        offset[None] >= 0.0, jnp.exp(-slopes[:, None, None] * jnp.maximum(offset, 0.0)[None]), 0.0
    )
    scores = jnp.einsum("cthe,cshe->chts", query, key_part, preferred_element_type=jnp.float32)
    weights = (scores * decays[None]).astype(jnp.bfloat16)
    within = jnp.einsum("chts,cshe->cthe", weights, value_part, preferred_element_type=jnp.float32)
    leading = jnp.exp(-slopes[None, :] * (places[:, None] + 1.0))
    scaled = query.astype(jnp.float32) * leading[None, :, :, None]
    carried = jnp.einsum("cthe,chef->cthf", scaled, start, precision=HIGHEST)
    lens_f = lens.astype(jnp.float32)
    active = (places[None, :] < lens_f[:, None]).astype(jnp.float32)
    attended = ((within + carried) * active[:, :, None, None]).astype(jnp.bfloat16)
    remain = lens_f[:, None] - 1.0 - places[None, :]
    trailing = jnp.where(
        remain[:, :, None] >= 0.0,
        jnp.exp(-slopes[None, None, :] * jnp.maximum(remain, 0.0)[:, :, None]),
        0.0,
    )
    weighted_keys = key_part.astype(jnp.float32) * trailing[..., None]
    update = jnp.einsum(
        "cshe,cshf->chef", weighted_keys, value_part.astype(jnp.float32), precision=HIGHEST
    )
    fading = jnp.exp(-slopes[None, :] * lens_f[:, None])
    states = fading[:, :, None, None] * start + update
    return (attended, states)


def body(queries, key_rows, value_rows, slopes, norm_gain, parents, lengths, parent_states):
    groups = lax.axis_size("expert")
    heads_all = slopes.shape[0]
    per_device = parent_states.shape[1]
    head_dim = parent_states.shape[-1]
    length_seg = queries.shape[0]
    piece = lax.all_gather(parent_states, "dp", axis=0, tiled=True)
    places = jnp.arange(piece.shape[0], dtype=jnp.int32)
    select = (parents[:, None] == places[None, :]).astype(jnp.float32)
    starting = jnp.einsum("cp,phef->chef", select, piece, precision=HIGHEST)
    query_rows = queries.reshape(length_seg, heads_all, head_dim)
    key_three = key_rows.reshape(length_seg, heads_all, head_dim)
    value_three = value_rows.reshape(length_seg, heads_all, head_dim)
    moved = (
        lax.all_to_all(query_rows, "expert", split_axis=1, concat_axis=0, tiled=True),
        lax.all_to_all(key_three, "expert", split_axis=1, concat_axis=0, tiled=True),
        lax.all_to_all(value_three, "expert", split_axis=1, concat_axis=0, tiled=True),
    )
    blocks = [part.reshape(groups, length_seg, per_device, head_dim) for part in moved]
    local_slopes = lax.dynamic_slice_in_dim(
        slopes, lax.axis_index("expert") * per_device, per_device
    )
    attended, child_states = lightning(
        blocks[0], blocks[1], blocks[2], starting, lengths, local_slopes
    )
    rows_out = lax.all_to_all(
        attended.reshape(groups * length_seg, per_device, head_dim),
        "expert",
        split_axis=0,
        concat_axis=1,
        tiled=True,
    )
    rows_flat = rows_out.reshape(length_seg, heads_all * head_dim).astype(jnp.float32)
    square_mean = jnp.mean(rows_flat * rows_flat, axis=-1, keepdims=True)
    mixed = (rows_flat * lax.rsqrt(square_mean + EPS) * norm_gain).astype(jnp.bfloat16)
    return (mixed, child_states)


def solution(mesh):
    in_specs = (
        P(("dp", "expert"), None),
        P(("dp", "expert"), None),
        P(("dp", "expert"), None),
        P(),
        P(),
        P("dp"),
        P("dp"),
        P("dp", "expert", None, None),
    )
    out_specs = (P(("dp", "expert"), None), P("dp", "expert", None, None))
    return jax.shard_map(body, mesh=mesh, in_specs=in_specs, out_specs=out_specs, check_vma=False)
```

profile of v0, /device:TPU:1, one launch (start us, length us, event | category | flops | bytes accessed | tf_op | source)
XLA Modules:
  0.0 294.5 jit_solution(13483779811316388971)
XLA Ops:
  7.2 1.6 copy-done
  8.8 1.9 copy_bitcast_fusion.1
  10.7 10.0 %all-to-all-start.1 = ((bf16[256,32,128]{2,0,1:T(8,128)(2,1)}), bf16[256,32,128]{2,0,1:T(8,128)(2,1)}, u32[]{:S(2)}, u32[]{:S(2)}) async-start(bf16[256,32,128]{2,0,1:T(8,128)(2,1)} %copy_bitcast_fusion.1), calls=%async_computation.1 | async-start | bytes 4194304 | tf_op jit(solution)/shard_map/all_to_all | solution.py:56
  20.7 0.7 all-gather.2.cloned.1.call-update
  21.4 3.5 %copy_bitcast_fusion = bf16[256,32,128]{2,0,1:T(8,128)(2,1)} fusion(bf16[256,4096]{1,0:T(8,128)(2,1)} %param.10), kind=kLoop, calls=%fused_computation.19 | loop fusion | bytes 4194304 | tf_op jit(solution)/shard_map/reshape | solution.py:53
  24.9 44.8 %all-to-all-done.1 = bf16[256,32,128]{2,0,1:T(8,128)(2,1)} async-done(((bf16[256,32,128]{2,0,1:T(8,128)(2,1)}), bf16[256,32,128]{2,0,1:T(8,128)(2,1)}, u32[]{:S(2)}, u32[]{:S(2)}) %all-to-all-start.1) | async-done | bytes 2097184 | tf_op jit(solution)/shard_map/all_to_all | solution.py:56
  69.7 5.0 %all-to-all-start.2 = ((bf16[256,32,128]{2,0,1:T(8,128)(2,1)}), bf16[256,32,128]{2,0,1:T(8,128)(2,1)}, u32[]{:S(2)}, u32[]{:S(2)}) async-start(bf16[256,32,128]{2,0,1:T(8,128)(2,1)} %copy_bitcast_fusion), calls=%async_computation.2 | async-start | bytes 4194304 | tf_op jit(solution)/shard_map/all_to_all | solution.py:57
  74.7 3.6 %copy_bitcast_fusion.2 = bf16[256,32,128]{2,0,1:T(8,128)(2,1)} fusion(bf16[256,4096]{1,0:T(8,128)(2,1)} %param.8), kind=kLoop, calls=%fused_computation.21 | loop fusion | bytes 4194304 | tf_op jit(solution)/shard_map/reshape | solution.py:51
  78.2 45.5 %all-to-all-done.2 = bf16[256,32,128]{2,0,1:T(8,128)(2,1)} async-done(((bf16[256,32,128]{2,0,1:T(8,128)(2,1)}), bf16[256,32,128]{2,0,1:T(8,128)(2,1)}, u32[]{:S(2)}, u32[]{:S(2)}) %all-to-all-start.2) | async-done | bytes 2097184 | tf_op jit(solution)/shard_map/all_to_all | solution.py:57
  123.7 5.0 %all-to-all-start = ((bf16[256,32,128]{2,0,1:T(8,128)(2,1)}), bf16[256,32,128]{2,0,1:T(8,128)(2,1)}, u32[]{:S(2)}, u32[]{:S(2)}) async-start(bf16[256,32,128]{2,0,1:T(8,128)(2,1)} %copy_bitcast_fusion.2), calls=%async_computation | async-start | bytes 4194304 | tf_op jit(solution)/shard_map/all_to_all | solution.py:55
  128.7 0.1 dynamic-slice_negate_fusion
  128.8 0.1 fusion.20
  129.0 0.1 multiply_exponential_fusion.1
  129.1 0.1 fusion.22
  129.2 0.1 fusion.21
  129.4 0.1 exponential_select_fusion.1
  129.5 0.2 exponential_select_fusion
  129.6 8.2 %fusion.7 = f32[16,2,128,128]{3,2,1,0:T(8,128)} fusion(bf16[16,256,2,128]{3,1,2,0:T(8,128)(2,1)} %bitcast.5, bf16[16,256,2,128]{3,1,2,0:T(8,128)(2,1)} %bitcast.3, f32[16,256,2]{1,2,0:T(2,128)S(1)} %exponential_select_fusion.1), kind=kOutput, calls=%fused_computation.10 | convolution fusion | flops 1612709888 | bytes 6324224 | tf_op jit(solution)/shard_map/cshe,cshf->chef/dot_general | solution.py:33
  137.9 9.8 %copy_add_fusion = (f32[16,2,128,128]{3,0,2,1:T(8,128)}, f32[16,2,128,128]{3,0,2,1:T(8,128)}) fusion(f32[16,2,128,128]{3,2,1,0:T(8,128)} %fusion.7, f32[16,2]{0,1:T(2,128)S(1)} %multiply_exponential_fusion.1, f32[32,2,128,128]{3,2,1,0:T(8,128)} %all-gather.2.cloned.1.call-done, s32[16]{0:T(128)S(1)} %copy-done.2), kind=kOutput, calls=%fused_computation.22 | convolution fusion | flops 202375680 | bytes 10485952 | tf_op jit(solution)/shard_map/cp,phef->chef/dot_general | solution.py:50
  147.7 30.1 %all-to-all-done = bf16[256,32,128]{2,0,1:T(8,128)(2,1)} async-done(((bf16[256,32,128]{2,0,1:T(8,128)(2,1)}), bf16[256,32,128]{2,0,1:T(8,128)(2,1)}, u32[]{:S(2)}, u32[]{:S(2)}) %all-to-all-start) | async-done | bytes 2097184 | tf_op jit(solution)/shard_map/all_to_all | solution.py:55
  177.8 9.1 %fusion.10 = f32[16,2,128,256]{2,3,1,0:T(8,128)} fusion(bf16[16,256,2,128]{3,1,2,0:T(8,128)(2,1)} %bitcast.1, f32[16,2,128,128]{3,0,2,1:T(8,128)} %get-tuple-element.13, f32[256,2]{0,1:T(2,128)S(1)} %multiply_exponential_fusion), kind=kOutput, calls=%fused_computation.14 | convolution fusion | flops 1612709888 | bytes 8390656 | tf_op jit(solution)/shard_map/cthe,chef->cthf/dot_general | solution.py:22
  186.9 7.8 %fusion.4 = bf16[16,256,2,128]{3,1,2,0:T(8,128)(2,1)} fusion(f32[16,2,128,256]{2,3,1,0:T(8,128)} %fusion.10, f32[16,256]{1,0:T(8,128)S(1)} %fusion.23, bf16[16,256,2,128]{3,1,2,0:T(8,128)(2,1)} %bitcast.5, f32[2,256,256]{2,1,0:T(8,128)S(1)} %exponential_select_fusion, bf16[16,256,2,128]{3,1,2,0:T(8,128)(2,1)} %bitcast.1, bf16[16,256,2,128]{3,1,2,0:T(8,128)(2,1)} %bitcast.3), kind=kOutput, calls=%fused_computation.7 | convolution fusion | flops 1081081856 | bytes 13123584 | tf_op jit(solution)/shard_map/chts,cshe->cthe/dot_general | solution.py:19
  194.6 1.7 copy.59
  196.4 18.1 %copy.60 = bf16[4096,2,128]{2,1,0:T(2,128)(2,1)} copy(bf16[4096,2,128]{2,0,1:T(8,128)(2,1)S(1)} %bitcast.54) | data formatting | bytes 4194304 | tf_op jit(solution)/shard_map/reshape | solution.py:67
  214.5 5.0 %all-to-all-start.3 = ((bf16[4096,2,128]{2,1,0:T(2,128)(2,1)}), bf16[4096,2,128]{2,1,0:T(2,128)(2,1)}, u32[]{:S(2)}, u32[]{:S(2)}) async-start(bf16[4096,2,128]{2,1,0:T(2,128)(2,1)} %copy.60), calls=%async_computation.3 | async-start | bytes 4194304 | tf_op jit(solution)/shard_map/all_to_all | solution.py:66
  219.5 3.6 %copy.66 = f32[16,2,128,128]{3,2,1,0:T(8,128)} copy(f32[16,2,128,128]{3,0,2,1:T(8,128)} %get-tuple-element.12) | data formatting | bytes 4194304
  223.1 45.5 %all-to-all-done.3 = bf16[4096,2,128]{2,1,0:T(2,128)(2,1)} async-done(((bf16[4096,2,128]{2,1,0:T(2,128)(2,1)}), bf16[4096,2,128]{2,1,0:T(2,128)(2,1)}, u32[]{:S(2)}, u32[]{:S(2)}) %all-to-all-start.3) | async-done | bytes 2097184 | tf_op jit(solution)/shard_map/all_to_all | solution.py:66
  268.5 3.8 %copy_convert_fusion = f32[4096,2,128]{2,0,1:T(8,128)} fusion(bf16[4096,2,128]{2,1,0:T(2,128)(2,1)} %all-to-all-done.3), kind=kLoop, calls=%fused_computation.23 | loop fusion | flops 1048576 | bytes 6291456 | tf_op jit(solution)/shard_map/convert_element_type | solution.py:73
  272.4 5.4 %copy.62 = f32[256,16,2,128]{0,3,2,1:T(8,128)} copy(f32[256,16,2,128]{3,0,1,2:T(8,128)} %bitcast.53) | data formatting | bytes 8388608 | tf_op jit(solution)/shard_map/convert_element_type | solution.py:73
  277.7 2.2 multiply_reduce_fusion
  280.0 3.6 %fusion.2 = bf16[256,4096]{0,1:T(8,128)(2,1)} fusion(f32[256,16,2,128]{0,3,2,1:T(8,128)} %copy.62, f32[4096]{0:T(1024)S(1)} %copy-done.1, f32[256]{0:T(256)S(1)} %add_rsqrt_fusion), kind=kLoop, calls=%fused_computation.4 | loop fusion | flops 3145728 | bytes 6308864 | tf_op jit(solution)/shard_map/convert_element_type | solution.py:75
  283.6 4.1 %copy.65 = bf16[256,4096]{1,0:T(8,128)(2,1)} copy(bf16[256,4096]{0,1:T(8,128)(2,1)} %fusion.2) | data formatting | bytes 4194304
  (20 shorter events, 0.3 us)
Async XLA Ops:
  7.2 1.6 copy-start
  10.7 59.0 %all-to-all-start.1 = ((bf16[256,32,128]{2,0,1:T(8,128)(2,1)}), bf16[256,32,128]{2,0,1:T(8,128)(2,1)}, u32[]{:S(2)}, u32[]{:S(2)}) async-start(bf16[256,32,128]{2,0,1:T(8,128)(2,1)} %copy_bitcast_fusion.1), calls=%async_computation.1 | async-start | bytes 4194304 | tf_op jit(solution)/shard_map/all_to_all | solution.py:56
  20.6 117.2 %all-gather.2.cloned.1.call-start = ((), (), s32[]{:S(2)}) async-start(), calls=%async_computation.4 | async-start | bytes 4456448 | tf_op jit(solution)/shard_map/all_gather | solution.py:47
  69.7 54.0 %all-to-all-start.2 = ((bf16[256,32,128]{2,0,1:T(8,128)(2,1)}), bf16[256,32,128]{2,0,1:T(8,128)(2,1)}, u32[]{:S(2)}, u32[]{:S(2)}) async-start(bf16[256,32,128]{2,0,1:T(8,128)(2,1)} %copy_bitcast_fusion), calls=%async_computation.2 | async-start | bytes 4194304 | tf_op jit(solution)/shard_map/all_to_all | solution.py:57
  78.2 50.5 %copy-start.4 = (s32[16]{0:T(128)S(1)}, s32[16]{0:T(128)}, u32[]{:S(2)}) copy-start(s32[16]{0:T(128)} %param.14) | copy-start | bytes 196
  78.2 50.5 %copy-start.3 = (f32[32]{0:T(128)S(1)}, f32[32]{0:T(128)}, u32[]{:S(2)}) copy-start(f32[32]{0:T(128)} %param.11) | copy-start | bytes 388
  123.7 54.0 %all-to-all-start = ((bf16[256,32,128]{2,0,1:T(8,128)(2,1)}), bf16[256,32,128]{2,0,1:T(8,128)(2,1)}, u32[]{:S(2)}, u32[]{:S(2)}) async-start(bf16[256,32,128]{2,0,1:T(8,128)(2,1)} %copy_bitcast_fusion.2), calls=%async_computation | async-start | bytes 4194304 | tf_op jit(solution)/shard_map/all_to_all | solution.py:55
  129.6 8.2 %copy-start.2 = (s32[16]{0:T(128)S(1)}, s32[16]{0:T(128)}, u32[]{:S(2)}) copy-start(s32[16]{0:T(128)} %param.13) | copy-start | bytes 196
  214.5 54.0 %all-to-all-start.3 = ((bf16[4096,2,128]{2,1,0:T(2,128)(2,1)}), bf16[4096,2,128]{2,1,0:T(2,128)(2,1)}, u32[]{:S(2)}, u32[]{:S(2)}) async-start(bf16[4096,2,128]{2,1,0:T(2,128)(2,1)} %copy.60), calls=%async_computation.3 | async-start | bytes 4194304 | tf_op jit(solution)/shard_map/all_to_all | solution.py:66
  277.7 2.3 copy-start.1
Sparse Core Ops, SparseCore 0:
  23.9 57.5 all-gather.1
where the time goes:
time: 295 us
  waiting for transfers between devices  167 us (57%)
  local copies, waits for them, and re-layouts  43.4 us (15%)
  matrix products  34.9 us (12%)
  starting transfers between devices  25 us (8%)
  between operations  14.1 us (5%)
  other arithmetic  10.5 us (4%)
    all_to_all x1, waiting for transfers between devices, body(): lax.all_to_all(value_three, 'expert', split_axis=1, concat_axis=0, tiled=...  45.5 us
    all_to_all x1, waiting for transfers between devices, body(): lax.all_to_all(attended.reshape(groups * length_seg, per_device, head_dim...  45.5 us
    all_to_all x1, waiting for transfers between devices, body(): lax.all_to_all(key_three, 'expert', split_axis=1, concat_axis=0, tiled=True)  44.8 us
    all_to_all x1, waiting for transfers between devices, body(): lax.all_to_all(query_rows, 'expert', split_axis=1, concat_axis=0, tiled=T...  30.1 us
    reshape x1, local copies, waits for them, and re-layouts, body(): attended.reshape(groups * length_seg, per_device, head_dim)  18.1 us
    all_to_all x1, starting transfers between devices, body(): lax.all_to_all(key_three, 'expert', split_axis=1, concat_axis=0, tiled=True)  9.98 us
    dot_general x1, matrix products, body(): starting = jnp.einsum('cp,phef->chef', select, piece, precision=HIGHEST)  9.82 us
    unnamed x12, local copies, waits for them, and re-layouts  9.26 us
  transfers between devices with their start and end apart: 5, of which 4 were waited for; matrix products, arithmetic and copies ran while one was open for 10% of the time, Pallas kernels for 0%

commit v1 on v0

v1 whole, which is shorter than its diff:
```python
import jax
import jax.numpy as jnp
from jax import lax
from jax.experimental import pallas as pl
from jax.experimental.pallas import tpu as pltpu
from jax.sharding import PartitionSpec as P

EPS = 1e-06
MESH = pl.DeviceIdType.MESH
SIDE = 4
RING = 8
GROUP = 16
HEADS = 32
DIM = 128
SEG = 256
PAIR = 2 * DIM
CUTS = 4
FAR = 1e9


def ring_step(i):
    j = i // 2
    off = RING // 2 + ((j + 1) // 2) * (1 - 2 * (j % 2))
    return off, (i + 1) % 2


def exchange(
    q_hbm, k_hbm, v_hbm, slopes, parents, lengths, states,
    att_hbm, got_u, start_hbm,
    q, k, v, total, att, offsets, sent_u, bank, picked, got_s,
    load_sem, bank_send, bank_hop, bank_recv, u_send, u_recv, s_send, s_recv, out_sem, own_sem,
):
    me_d = lax.axis_index("dp")
    me_e = lax.axis_index("expert")
    y, x = me_d // SIDE, me_d % SIDE
    z, core = me_e // 2, me_e % 2

    arrays = ((k_hbm, k), (v_hbm, v), (q_hbm, q))

    def load(n, cut):
        rows = pl.ds(cut * (SEG // CUTS), SEG // CUTS)
        src, dst = arrays[n]
        return pltpu.make_async_copy(src.at[rows], dst.at[rows], load_sem.at[n, cut])

    for n in range(3):
        for cut in range(CUTS):
            load(n, cut).start()

    def along(head, j):
        return y * SIDE + (x + j) % SIDE if head == 0 else ((y + j) % SIDE) * SIDE + x

    barrier = pltpu.get_barrier_semaphore()

    def greet(i, _):
        pl.semaphore_signal(
            barrier, inc=1, device_id=(me_d, (me_e + i) % GROUP), device_id_type=MESH
        )
        return 0

    lax.fori_loop(1, GROUP, greet, 0)
    for head in range(2):
        for j in range(1, SIDE):
            pl.semaphore_signal(
                barrier, inc=1, device_id=(along(head, j), me_e), device_id_type=MESH
            )

    for head in range(2):
        for parent in range(2):
            bank[head, 2 * me_d + parent] = states[parent, head].astype(jnp.bfloat16)

    t_of = lax.broadcasted_iota(jnp.int32, (SEG, SEG), 0)
    s_of = lax.broadcasted_iota(jnp.int32, (SEG, SEG), 1)
    offsets[...] = jnp.where(t_of >= s_of, (t_of - s_of).astype(jnp.float32), FAR)

    length = lengths[me_e]
    place = lax.broadcasted_iota(jnp.int32, (SEG, DIM), 0)
    remain = (length - 1 - place).astype(jnp.float32)
    inside = place < length
    step_of = (place + 1).astype(jnp.float32)

    pl.semaphore_wait(barrier, GROUP - 1 + 2 * (SIDE - 1))

    def block(head, d):
        return bank.at[head, pl.ds(2 * d, 2)]

    def bank_copy(head, d, to, sem):
        return pltpu.make_async_remote_copy(
            src_ref=block(head, d), dst_ref=block(head, d), send_sem=sem,
            recv_sem=bank_recv.at[head, d], device_id=(to, me_e), device_id_type=MESH,
        )

    def first_hop(head, j):
        return bank_copy(head, me_d, along(head, j), bank_send.at[head, j - 1])

    def second_hop(head, b, j):
        return bank_copy(head, along(head, b), along(1 - head, j), bank_hop.at[head, b, j - 1])

    for head in range(2):
        for j in range(1, SIDE):
            first_hop(head, j).start()
    for head in range(2):
        for j in range(1, SIDE):
            second_hop(head, 0, j).start()

    for cut in range(CUTS):
        load(0, cut).wait()
        load(1, cut).wait()

    def columns(e):
        return pl.ds(pl.multiple_of(e * PAIR, PAIR), PAIR)

    def head_columns(e, head):
        return pl.ds(pl.multiple_of(e * PAIR + head * DIM, DIM), DIM)

    def partner(i):
        off, flip = ring_step(i)
        return 2 * ((z + off) % RING) + (core + flip) % 2

    def source(i):
        off, flip = ring_step(i)
        return 2 * ((z + RING - off) % RING) + (core + flip) % 2

    def send_u(e):
        return pltpu.make_async_remote_copy(
            src_ref=sent_u.at[e], dst_ref=got_u.at[me_e], send_sem=u_send.at[e],
            recv_sem=u_recv.at[me_e], device_id=(me_d, e), device_id_type=MESH,
        )

    def recv_u(e):
        return pltpu.make_async_remote_copy(
            src_ref=sent_u.at[e], dst_ref=got_u.at[e], send_sem=u_send.at[e],
            recv_sem=u_recv.at[e], device_id=(me_d, e), device_id_type=MESH,
        )

    def send_s(e):
        return pltpu.make_async_remote_copy(
            src_ref=picked.at[e], dst_ref=got_s.at[me_e], send_sem=s_send.at[e],
            recv_sem=s_recv.at[me_e], device_id=(me_d, e), device_id_type=MESH,
        )

    def recv_s(e):
        return pltpu.make_async_remote_copy(
            src_ref=picked.at[e], dst_ref=got_s.at[e], send_sem=s_send.at[e],
            recv_sem=s_recv.at[e], device_id=(me_d, e), device_id_type=MESH,
        )

    def update(e):
        for head in range(2):
            cols = head_columns(e, head)
            slope = slopes[2 * e + head]
            fade = jnp.where(remain >= 0.0, jnp.exp(-slope * jnp.maximum(remain, 0.0)), 0.0)
            keys = (k[:, cols].astype(jnp.float32) * fade).astype(jnp.bfloat16)
            sent_u[e, head] = lax.dot_general(
                keys, v[:, cols], (((0,), (0,)), ((), ())), preferred_element_type=jnp.float32
            ).astype(jnp.bfloat16)

    def update_step(i, _):
        e = partner(i)
        update(e)
        send_u(e).start()
        return 0

    lax.fori_loop(0, GROUP - 1, update_step, 0)
    update(me_e)
    own_u = pltpu.make_async_copy(sent_u.at[me_e], got_u.at[me_e], own_sem.at[0])
    own_u.start()

    for b in range(1, SIDE):
        for head in range(2):
            d = along(head, b)
            bank_copy(head, d, d, bank_send.at[head, 0]).wait_recv()
            for j in range(1, SIDE):
                second_hop(head, b, j).start()

    for cut in range(CUTS):
        load(2, cut).wait()

    def within(i, _):
        cols = pl.ds(pl.multiple_of(i * DIM, DIM), DIM)
        decay = jnp.exp(-slopes[i] * offsets[...])
        scores = lax.dot_general(
            q[:, cols], k[:, cols], (((1,), (1,)), ((), ())), preferred_element_type=jnp.float32
        )
        total[:, cols] = jnp.dot(
            (scores * decay).astype(jnp.bfloat16), v[:, cols], preferred_element_type=jnp.float32
        )
        return 0

    lax.fori_loop(0, HEADS, within, 0)

    for j in range(1, SIDE):
        for b in range(SIDE):
            d = ((y + j) % SIDE) * SIDE + (x + b) % SIDE
            bank_copy(0, d, along(0, 1), bank_send.at[0, 0]).wait_recv()
            d = ((y + b) % SIDE) * SIDE + (x + j) % SIDE
            bank_copy(1, d, along(0, 1), bank_send.at[0, 0]).wait_recv()

    def pick(e):
        parent = parents[e]
        for head in range(2):
            picked[e, head] = bank[head, parent]

    def pick_step(i, _):
        e = partner(i)
        pick(e)
        send_s(e).start()
        return 0

    lax.fori_loop(0, GROUP - 1, pick_step, 0)
    pick(me_e)
    keep = pltpu.make_async_copy(picked, start_hbm, own_sem.at[1])
    keep.start()

    def att_out(e):
        return pltpu.make_async_copy(att.at[:, columns(e)], att_hbm.at[:, columns(e)], out_sem.at[e])

    def finish(e, src, at):
        for head in range(2):
            cols = head_columns(e, head)
            lead = jnp.exp(-slopes[2 * e + head] * step_of)
            carried = jnp.dot(q[:, cols], src[at, head], preferred_element_type=jnp.float32)
            att[:, cols] = jnp.where(inside, total[:, cols] + carried * lead, 0.0).astype(jnp.bfloat16)
        att_out(e).start()

    finish(me_e, picked, me_e)

    def finish_step(i, _):
        e = source(i)
        recv_s(e).wait_recv()
        finish(e, got_s, e)
        return 0

    lax.fori_loop(0, GROUP - 1, finish_step, 0)

    def drain(i, _):
        e = source(i)
        recv_u(e).wait_recv()
        send_u(e).wait_send()
        send_s(e).wait_send()
        att_out(e).wait()
        return 0

    lax.fori_loop(0, GROUP - 1, drain, 0)
    att_out(me_e).wait()
    own_u.wait()
    keep.wait()
    for head in range(2):
        for j in range(1, SIDE):
            first_hop(head, j).wait_send()
            for b in range(SIDE):
                second_hop(head, b, j).wait_send()


STEPS = 8
TOKENS = SEG // STEPS
KIDS = GROUP // STEPS


def settle(att, got_u, start, slopes, lengths, gain, mixed, child):
    me_e = lax.axis_index("expert")
    at = pl.program_id(0)
    rows = att[...].astype(jnp.float32)
    mean = jnp.mean(rows * rows, axis=-1, keepdims=True)
    mixed[...] = (rows * lax.rsqrt(mean + EPS) * gain[...]).astype(jnp.bfloat16)
    for kid in range(KIDS):
        length = lengths[at * KIDS + kid].astype(jnp.float32)
        for head in range(2):
            slope = slopes[2 * me_e + head]
            fade = jnp.exp(jnp.full((DIM, DIM), -slope * length, jnp.float32))
            child[kid, head] = fade * start[kid, head].astype(jnp.float32) + got_u[
                kid, head
            ].astype(jnp.float32)


def body(queries, key_rows, value_rows, slopes, norm_gain, parents, lengths, parent_states):
    anywhere = pl.BlockSpec(memory_space=pl.ANY)
    smem = pl.BlockSpec(memory_space=pltpu.SMEM)
    vmem = pl.BlockSpec(memory_space=pltpu.VMEM)
    dma = pltpu.SemaphoreType.DMA
    bf16, f32 = jnp.bfloat16, jnp.float32
    width = HEADS * DIM
    moved = (GROUP, 2, DIM, DIM)
    att, got_u, start = pl.pallas_call(
        exchange,
        out_shape=(
            jax.ShapeDtypeStruct((SEG, width), bf16),
            jax.ShapeDtypeStruct(moved, bf16),
            jax.ShapeDtypeStruct(moved, bf16),
        ),
        in_specs=[anywhere] * 3 + [smem] * 3 + [vmem],
        out_specs=(anywhere,) * 3,
        scratch_shapes=[
            pltpu.VMEM((SEG, width), bf16),
            pltpu.VMEM((SEG, width), bf16),
            pltpu.VMEM((SEG, width), bf16),
            pltpu.VMEM((SEG, width), f32),
            pltpu.VMEM((SEG, width), bf16),
            pltpu.VMEM((SEG, SEG), f32),
            pltpu.VMEM(moved, bf16),
            pltpu.VMEM((2, 2 * SIDE * SIDE, DIM, DIM), bf16),
            pltpu.VMEM(moved, bf16),
            pltpu.VMEM(moved, bf16),
            dma((3, CUTS)),
            dma((2, SIDE - 1)),
            dma((2, SIDE, SIDE - 1)),
            dma((2, SIDE * SIDE)),
            dma((GROUP,)),
            dma((GROUP,)),
            dma((GROUP,)),
            dma((GROUP,)),
            dma((GROUP,)),
            dma((2,)),
        ],
        compiler_params=pltpu.CompilerParams(
            collective_id=0, has_side_effects=True, vmem_limit_bytes=40 * 1024 * 1024
        ),
        name="exchange",
    )(queries, key_rows, value_rows, slopes, parents, lengths, parent_states)
    mixed, child = pl.pallas_call(
        settle,
        grid=(STEPS,),
        out_shape=(
            jax.ShapeDtypeStruct((SEG, width), bf16),
            jax.ShapeDtypeStruct(moved, f32),
        ),
        in_specs=[
            pl.BlockSpec((TOKENS, width), lambda i: (i, 0)),
            pl.BlockSpec((KIDS, 2, DIM, DIM), lambda i: (i, 0, 0, 0)),
            pl.BlockSpec((KIDS, 2, DIM, DIM), lambda i: (i, 0, 0, 0)),
            smem,
            smem,
            pl.BlockSpec((1, width), lambda i: (0, 0)),
        ],
        out_specs=(
            pl.BlockSpec((TOKENS, width), lambda i: (i, 0)),
            pl.BlockSpec((KIDS, 2, DIM, DIM), lambda i: (i, 0, 0, 0)),
        ),
        compiler_params=pltpu.CompilerParams(vmem_limit_bytes=32 * 1024 * 1024),
        name="settle",
    )(att, got_u, start, slopes, lengths, norm_gain.reshape(1, width))
    return mixed, child


def solution(mesh):
    in_specs = (
        P(("dp", "expert"), None),
        P(("dp", "expert"), None),
        P(("dp", "expert"), None),
        P(),
        P(),
        P("dp"),
        P("dp"),
        P("dp", "expert", None, None),
    )
    out_specs = (P(("dp", "expert"), None), P("dp", "expert", None, None))
    return jax.shard_map(body, mesh=mesh, in_specs=in_specs, out_specs=out_specs, check_vma=False)
```

time: 295 us -> 73.7 us (0.25)
  waiting for transfers between devices: 167 us -> 0 us
  Pallas kernels: 0 us -> 65.1 us
  local copies, waits for them, and re-layouts: 43.4 us -> 7.68 us
  matrix products: 34.9 us -> 0 us
  starting transfers between devices: 25 us -> 0 us
  between operations: 14.1 us -> 0.66 us
  other arithmetic: 10.5 us -> 0 us
    all_to_all x4 -> x0, waiting for transfers between devices: 166 us -> none  [the longest x1 45.5 us: body(): lax.all_to_all(value_three, 'expert', split_axis=1, concat_axis=0, tiled=...]
    pallas_call x0 -> x2, Pallas kernels: none -> 65.1 us  [the longest x1 60.4 us: body(): pl.pallas_call(exchange, out_shape=(jax.ShapeDtypeStruct((SEG, width), bf...]
    dot_general x4 -> x0, matrix products: 34.9 us -> none  [the longest x1 9.82 us: body(): starting = jnp.einsum('cp,phef->chef', select, piece, precision=HIGHEST)]
    reshape x4 -> x0, local copies, waits for them, and re-layouts: 27.1 us -> none  [the longest x1 18.1 us: body(): attended.reshape(groups * length_seg, per_device, head_dim)]
    all_to_all x4 -> x0, starting transfers between devices: 24.9 us -> none  [the longest x1 9.98 us: body(): lax.all_to_all(key_three, 'expert', split_axis=1, concat_axis=0, tiled=True)]
    convert_element_type x4 -> x0, other arithmetic: 7.48 us -> none  [the longest x1 3.83 us: body(): rows_out.reshape(length_seg, heads_all * head_dim).astype(jnp.float32)]
    convert_element_type x2 -> x0, local copies, waits for them, and re-layouts: 7.11 us -> none  [the longest x1 5.38 us: body(): rows_out.reshape(length_seg, heads_all * head_dim).astype(jnp.float32)]
    unnamed x12 -> x16, local copies, waits for them, and re-layouts: 9.26 us -> 7.68 us
  transfers between devices with their start and end apart: 5 -> 0, of which waited for: 4 -> 0; matrix products, arithmetic and copies ran while one was open for 10% -> 0% of each run, Pallas kernels for 0% -> 0%
where the time goes in v1:
time: 73.7 us; the launch traced here: 73.4 us
  Pallas kernels  65.1 us (88%)
  local copies, waits for them, and re-layouts  7.68 us (10%)
    pallas_call x1, Pallas kernels, body(): pl.pallas_call(exchange, out_shape=(jax.ShapeDtypeStruct((SEG, width), bf...  60.4 us
    unnamed x16, local copies, waits for them, and re-layouts  7.68 us
    pallas_call x1, Pallas kernels, body(): pl.pallas_call(settle, grid=(STEPS,), out_shape=(jax.ShapeDtypeStruct((SE...  4.69 us

profile of v1, /device:TPU:1, one launch (start us, length us, event | category | flops | bytes accessed | tf_op | source)
XLA Modules:
  0.0 73.4 jit_solution(18341652745558780664)
XLA Ops:
  0.6 0.0 copy-start
  0.6 1.6 %copy-done = bf16[256,4096]{1,0:T(8,128)(2,1)S(1)} copy-done((bf16[256,4096]{1,0:T(8,128)(2,1)S(1)}, bf16[256,4096]{1,0:T(8,128)(2,1)}, u32[]{:S(2)}) %copy-start) | copy-done | bytes 2097176
  2.2 0.0 copy-start.1
  2.2 1.6 %copy-done.1 = bf16[256,4096]{1,0:T(8,128)(2,1)S(1)} copy-done((bf16[256,4096]{1,0:T(8,128)(2,1)S(1)}, bf16[256,4096]{1,0:T(8,128)(2,1)}, u32[]{:S(2)}) %copy-start.1) | copy-done | bytes 2097176
  3.8 0.0 copy-start.2
  3.8 1.6 %copy-done.2 = bf16[256,4096]{1,0:T(8,128)(2,1)S(1)} copy-done((bf16[256,4096]{1,0:T(8,128)(2,1)S(1)}, bf16[256,4096]{1,0:T(8,128)(2,1)}, u32[]{:S(2)}) %copy-start.2) | copy-done | bytes 2097176
  5.4 0.0 copy-start.3
  5.4 0.9 %copy-done.3 = f32[2,2,128,128]{3,2,1,0:T(8,128)S(1)} copy-done((f32[2,2,128,128]{3,2,1,0:T(8,128)S(1)}, f32[2,2,128,128]{3,2,1,0:T(8,128)}, u32[]{:S(2)}) %copy-start.3) | copy-done | bytes 262168
  6.4 0.0 copy-start.5
  6.4 0.7 copy-done.5
  7.0 0.0 copy-start.6
  7.0 0.7 copy-done.6
  7.7 0.0 copy-start.7
  7.7 0.7 copy-done.7
  8.3 0.0 copy-start.4
  8.3 60.4 %exchange.1 = (bf16[256,4096]{1,0:T(8,128)(2,1)S(1)}, bf16[16,2,128,128]{3,2,1,0:T(8,128)(2,1)S(1)}, bf16[16,2,128,128]{3,2,1,0:T(8,128)(2,1)S(1)}) custom-call(bf16[256,4096]{1,0:T(8,128)(2,1)S(1)} %copy-done, bf16[256,4096]{1,0:T(8,128)(2,1)S(1)} %copy-done.1, bf16[256,4096]{1,0:T(8,128)(2,1)S(1)} %copy-done.2, f32[32]{0:T(128)S(1)} %copy-done.5, ...), custom_call_target="tpu_custom_call" | custom-call | tf_op jit(solution)/shard_map/exchange/pallas_call | solution.py:283
  68.7 0.0 copy-done.4
  68.7 4.7 %settle.1 = (bf16[256,4096]{1,0:T(8,128)(2,1)}, f32[16,2,128,128]{3,2,1,0:T(8,128)}) custom-call(bf16[256,4096]{1,0:T(8,128)(2,1)S(1)} %get-tuple-element.5.att, bf16[16,2,128,128]{3,2,1,0:T(8,128)(2,1)S(1)} %get-tuple-element.6.got_u, bf16[16,2,128,128]{3,2,1,0:T(8,128)(2,1)S(1)} %get-tuple-element.7.start, f32[32]{0:T(128)S(1)} %copy-done.5, ...), custom_call_target="tpu_custom_call" | custom-call | tf_op jit(solution)/shard_map/settle/pallas_call | solution.py:319
Async XLA Ops:
  0.6 1.6 %copy-start = (bf16[256,4096]{1,0:T(8,128)(2,1)S(1)}, bf16[256,4096]{1,0:T(8,128)(2,1)}, u32[]{:S(2)}) copy-start(bf16[256,4096]{1,0:T(8,128)(2,1)} %q_hbm.1) | copy-start | bytes 6291460
  2.2 1.6 %copy-start.1 = (bf16[256,4096]{1,0:T(8,128)(2,1)S(1)}, bf16[256,4096]{1,0:T(8,128)(2,1)}, u32[]{:S(2)}) copy-start(bf16[256,4096]{1,0:T(8,128)(2,1)} %k_hbm.1) | copy-start | bytes 6291460
  3.8 1.6 %copy-start.2 = (bf16[256,4096]{1,0:T(8,128)(2,1)S(1)}, bf16[256,4096]{1,0:T(8,128)(2,1)}, u32[]{:S(2)}) copy-start(bf16[256,4096]{1,0:T(8,128)(2,1)} %v_hbm.1) | copy-start | bytes 6291460
  5.4 0.9 %copy-start.3 = (f32[2,2,128,128]{3,2,1,0:T(8,128)S(1)}, f32[2,2,128,128]{3,2,1,0:T(8,128)}, u32[]{:S(2)}) copy-start(f32[2,2,128,128]{3,2,1,0:T(8,128)} %states.1) | copy-start | bytes 786436
  6.4 0.7 copy-start.5
  7.0 0.7 copy-start.6
  7.7 0.7 copy-start.7
  8.3 60.4 %copy-start.4 = (f32[4096]{0:T(1024)S(1)}, f32[4096]{0:T(1024)}, u32[]{:S(2)}) copy-start(f32[4096]{0:T(1024)} %param.12) | copy-start | bytes 49156

commit v2 on v1

v2 whole, which is shorter than its diff:
```python
import jax
import jax.numpy as jnp
from jax import lax
from jax.experimental import pallas as pl
from jax.experimental.pallas import tpu as pltpu
from jax.sharding import PartitionSpec as P

EPS = 1e-06
MESH = pl.DeviceIdType.MESH
SIDE = 4
RING = 8
GROUP = 16
HEADS = 32
DIM = 128
SEG = 256
PAIR = 2 * DIM
CUTS = 4
FAR = 1e9


def ring_step(i):
    j = i // 2
    off = RING // 2 + ((j + 1) // 2) * (1 - 2 * (j % 2))
    return off, (i + 1) % 2


def exchange(
    q_hbm, k_hbm, v_hbm, slopes_hbm, parents_hbm, lengths_hbm, states_hbm,
    att, got_u, picked,
    q, k, v, slopes, parents, lengths, states, total, offsets, sent_u, bank, got_s,
    load_sem, small_sem, bank_send, bank_hop, bank_recv, u_send, u_recv, s_send, s_recv, own_sem,
):
    me_d = lax.axis_index("dp")
    me_e = lax.axis_index("expert")
    y, x = me_d // SIDE, me_d % SIDE
    z, core = me_e // 2, me_e % 2

    arrays = ((k_hbm, k), (v_hbm, v), (q_hbm, q))

    def load(n, cut):
        rows = pl.ds(cut * (SEG // CUTS), SEG // CUTS)
        src, dst = arrays[n]
        return pltpu.make_async_copy(src.at[rows], dst.at[rows], load_sem.at[n, cut])

    smalls = [
        pltpu.make_async_copy(src, dst, small_sem.at[n])
        for n, (src, dst) in enumerate(
            ((states_hbm, states), (slopes_hbm, slopes), (lengths_hbm, lengths), (parents_hbm, parents))
        )
    ]
    for small in smalls:
        small.start()
    for n in range(3):
        for cut in range(CUTS):
            load(n, cut).start()

    def along(head, j):
        return y * SIDE + (x + j) % SIDE if head == 0 else ((y + j) % SIDE) * SIDE + x

    barrier = pltpu.get_barrier_semaphore()

    def greet(i, _):
        pl.semaphore_signal(
            barrier, inc=1, device_id=(me_d, (me_e + i) % GROUP), device_id_type=MESH
        )
        return 0

    lax.fori_loop(1, GROUP, greet, 0)
    for head in range(2):
        for j in range(1, SIDE):
            pl.semaphore_signal(
                barrier, inc=1, device_id=(along(head, j), me_e), device_id_type=MESH
            )

    for small in smalls:
        small.wait()

    for head in range(2):
        for parent in range(2):
            bank[head, 2 * me_d + parent] = states[parent, head].astype(jnp.bfloat16)

    t_of = lax.broadcasted_iota(jnp.int32, (SEG, SEG), 0)
    s_of = lax.broadcasted_iota(jnp.int32, (SEG, SEG), 1)
    offsets[...] = jnp.where(t_of >= s_of, (t_of - s_of).astype(jnp.float32), FAR)

    length = lengths[me_e]
    place = lax.broadcasted_iota(jnp.int32, (SEG, DIM), 0)
    remain = (length - 1 - place).astype(jnp.float32)
    inside = place < length
    step_of = (place + 1).astype(jnp.float32)

    def head_columns(e, head):
        return pl.ds(pl.multiple_of(e * PAIR + head * DIM, DIM), DIM)

    def partner(i):
        off, flip = ring_step(i)
        return 2 * ((z + off) % RING) + (core + flip) % 2

    def source(i):
        off, flip = ring_step(i)
        return 2 * ((z + RING - off) % RING) + (core + flip) % 2

    def update(e):
        for head in range(2):
            cols = head_columns(e, head)
            slope = slopes[2 * e + head]
            fade = jnp.where(remain >= 0.0, jnp.exp(-slope * jnp.maximum(remain, 0.0)), 0.0)
            keys = (k[:, cols].astype(jnp.float32) * fade).astype(jnp.bfloat16)
            sent_u[e, head] = lax.dot_general(
                keys, v[:, cols], (((0,), (0,)), ((), ())), preferred_element_type=jnp.float32
            ).astype(jnp.bfloat16)

    for cut in range(CUTS):
        load(0, cut).wait()
        load(1, cut).wait()
    update(partner(0))

    pl.semaphore_wait(barrier, GROUP - 1 + 2 * (SIDE - 1))

    def block(head, d):
        return bank.at[head, pl.ds(2 * d, 2)]

    def bank_copy(head, d, to, sem):
        return pltpu.make_async_remote_copy(
            src_ref=block(head, d), dst_ref=block(head, d), send_sem=sem,
            recv_sem=bank_recv.at[head, d], device_id=(to, me_e), device_id_type=MESH,
        )

    def first_hop(head, j):
        return bank_copy(head, me_d, along(head, j), bank_send.at[head, j - 1])

    def second_hop(head, b, j):
        return bank_copy(head, along(head, b), along(1 - head, j), bank_hop.at[head, b, j - 1])

    for head in range(2):
        for j in range(1, SIDE):
            first_hop(head, j).start()
    for head in range(2):
        for j in range(1, SIDE):
            second_hop(head, 0, j).start()

    def send_u(e):
        return pltpu.make_async_remote_copy(
            src_ref=sent_u.at[e], dst_ref=got_u.at[me_e], send_sem=u_send.at[e],
            recv_sem=u_recv.at[me_e], device_id=(me_d, e), device_id_type=MESH,
        )

    def recv_u(e):
        return pltpu.make_async_remote_copy(
            src_ref=sent_u.at[e], dst_ref=got_u.at[e], send_sem=u_send.at[e],
            recv_sem=u_recv.at[e], device_id=(me_d, e), device_id_type=MESH,
        )

    def send_s(e):
        return pltpu.make_async_remote_copy(
            src_ref=picked.at[e], dst_ref=got_s.at[me_e], send_sem=s_send.at[e],
            recv_sem=s_recv.at[me_e], device_id=(me_d, e), device_id_type=MESH,
        )

    def recv_s(e):
        return pltpu.make_async_remote_copy(
            src_ref=picked.at[e], dst_ref=got_s.at[e], send_sem=s_send.at[e],
            recv_sem=s_recv.at[e], device_id=(me_d, e), device_id_type=MESH,
        )

    def update_step(i, _):
        send_u(partner(i)).start()
        update(partner(i + 1))
        return 0

    lax.fori_loop(0, GROUP - 1, update_step, 0)
    own_u = pltpu.make_async_copy(sent_u.at[me_e], got_u.at[me_e], own_sem.at[0])
    own_u.start()

    for b in range(1, SIDE):
        for head in range(2):
            d = along(head, b)
            bank_copy(head, d, d, bank_send.at[head, 0]).wait_recv()
            for j in range(1, SIDE):
                second_hop(head, b, j).start()

    for cut in range(CUTS):
        load(2, cut).wait()

    def within(i, _):
        cols = pl.ds(pl.multiple_of(i * DIM, DIM), DIM)
        decay = jnp.exp(-slopes[i] * offsets[...])
        scores = lax.dot_general(
            q[:, cols], k[:, cols], (((1,), (1,)), ((), ())), preferred_element_type=jnp.float32
        )
        total[:, cols] = jnp.dot(
            (scores * decay).astype(jnp.bfloat16), v[:, cols], preferred_element_type=jnp.float32
        )
        return 0

    lax.fori_loop(0, HEADS, within, 0)

    for j in range(1, SIDE):
        for b in range(SIDE):
            d = ((y + j) % SIDE) * SIDE + (x + b) % SIDE
            bank_copy(0, d, along(0, 1), bank_send.at[0, 0]).wait_recv()
            d = ((y + b) % SIDE) * SIDE + (x + j) % SIDE
            bank_copy(1, d, along(0, 1), bank_send.at[0, 0]).wait_recv()

    def pick(e):
        parent = parents[e]
        for head in range(2):
            picked[e, head] = bank[head, parent]

    def pick_step(i, _):
        e = partner(i)
        pick(e)
        send_s(e).start()
        return 0

    lax.fori_loop(0, GROUP - 1, pick_step, 0)
    pick(me_e)

    def finish(e, src, at):
        for head in range(2):
            cols = head_columns(e, head)
            lead = jnp.exp(-slopes[2 * e + head] * step_of)
            carried = jnp.dot(q[:, cols], src[at, head], preferred_element_type=jnp.float32)
            att[:, cols] = jnp.where(inside, total[:, cols] + carried * lead, 0.0).astype(jnp.bfloat16)

    finish(me_e, picked, me_e)

    def finish_step(i, _):
        e = source(i)
        recv_s(e).wait_recv()
        finish(e, got_s, e)
        return 0

    lax.fori_loop(0, GROUP - 1, finish_step, 0)

    def drain(i, _):
        e = source(i)
        recv_u(e).wait_recv()
        send_u(e).wait_send()
        send_s(e).wait_send()
        return 0

    lax.fori_loop(0, GROUP - 1, drain, 0)
    own_u.wait()
    for head in range(2):
        for j in range(1, SIDE):
            first_hop(head, j).wait_send()
            for b in range(SIDE):
                second_hop(head, b, j).wait_send()


STEPS = 8
TOKENS = SEG // STEPS
KIDS = GROUP // STEPS


def settle(att, got_u, start, gain, slopes, lengths, mixed_hbm, child_hbm, mixed, child, sem):
    me_e = lax.axis_index("expert")

    def out(at):
        rows, kids = pl.ds(at * TOKENS, TOKENS), pl.ds(at * KIDS, KIDS)
        return (
            pltpu.make_async_copy(mixed.at[rows], mixed_hbm.at[rows], sem.at[0, at]),
            pltpu.make_async_copy(child.at[kids], child_hbm.at[kids], sem.at[1, at]),
        )

    def step(at, _):
        for kid in range(KIDS):
            length = lengths[at * KIDS + kid].astype(jnp.float32)
            for head in range(2):
                slope = slopes[2 * me_e + head]
                fade = jnp.exp(jnp.full((1, DIM), -slope * length, jnp.float32))
                child[at * KIDS + kid, head] = fade * start[at * KIDS + kid, head].astype(
                    jnp.float32
                ) + got_u[at * KIDS + kid, head].astype(jnp.float32)
        out(at)[1].start()
        here = pl.ds(pl.multiple_of(at * TOKENS, TOKENS), TOKENS)
        rows = att[here, :].astype(jnp.float32)
        mean = jnp.mean(rows * rows, axis=-1, keepdims=True)
        mixed[here, :] = (rows * lax.rsqrt(mean + EPS) * gain[...]).astype(jnp.bfloat16)
        out(at)[0].start()
        return 0

    lax.fori_loop(0, STEPS, step, 0)
    for at in range(STEPS):
        for copy in out(at):
            copy.wait()


def body(queries, key_rows, value_rows, slopes, norm_gain, parents, lengths, parent_states):
    anywhere = pl.BlockSpec(memory_space=pl.ANY)
    smem = pl.BlockSpec(memory_space=pltpu.SMEM)
    vmem = pl.BlockSpec(memory_space=pltpu.VMEM)
    dma = pltpu.SemaphoreType.DMA
    bf16, f32 = jnp.bfloat16, jnp.float32
    width = HEADS * DIM
    moved = (GROUP, 2, DIM, DIM)
    in_hbm = [
        pltpu.with_memory_space_constraint(a, pltpu.HBM)
        for a in (queries, key_rows, value_rows, slopes, parents, lengths, parent_states)
    ]
    att, got_u, start = pl.pallas_call(
        exchange,
        out_shape=(
            jax.ShapeDtypeStruct((SEG, width), bf16),
            jax.ShapeDtypeStruct(moved, bf16),
            jax.ShapeDtypeStruct(moved, bf16),
        ),
        in_specs=[anywhere] * 7,
        out_specs=(vmem,) * 3,
        scratch_shapes=[
            pltpu.VMEM((SEG, width), bf16),
            pltpu.VMEM((SEG, width), bf16),
            pltpu.VMEM((SEG, width), bf16),
            pltpu.SMEM((HEADS,), f32),
            pltpu.SMEM((GROUP,), jnp.int32),
            pltpu.SMEM((GROUP,), jnp.int32),
            pltpu.VMEM((2, 2, DIM, DIM), f32),
            pltpu.VMEM((SEG, width), f32),
            pltpu.VMEM((SEG, SEG), f32),
            pltpu.VMEM(moved, bf16),
            pltpu.VMEM((2, 2 * SIDE * SIDE, DIM, DIM), bf16),
            pltpu.VMEM(moved, bf16),
            dma((3, CUTS)),
            dma((4,)),
            dma((2, SIDE - 1)),
            dma((2, SIDE, SIDE - 1)),
            dma((2, SIDE * SIDE)),
            dma((GROUP,)),
            dma((GROUP,)),
            dma((GROUP,)),
            dma((GROUP,)),
            dma((1,)),
        ],
        compiler_params=pltpu.CompilerParams(
            collective_id=0, has_side_effects=True, vmem_limit_bytes=40 * 1024 * 1024
        ),
        name="exchange",
    )(*in_hbm)
    mixed, child = pl.pallas_call(
        settle,
        out_shape=(
            jax.ShapeDtypeStruct((SEG, width), bf16),
            jax.ShapeDtypeStruct(moved, f32),
        ),
        in_specs=[vmem] * 4 + [smem] * 2,
        out_specs=(anywhere,) * 2,
        scratch_shapes=[
            pltpu.VMEM((SEG, width), bf16),
            pltpu.VMEM(moved, f32),
            dma((2, STEPS)),
        ],
        compiler_params=pltpu.CompilerParams(vmem_limit_bytes=40 * 1024 * 1024),
        name="settle",
    )(att, got_u, start, norm_gain.reshape(1, width), slopes, lengths)
    return mixed, child


def solution(mesh):
    in_specs = (
        P(("dp", "expert"), None),
        P(("dp", "expert"), None),
        P(("dp", "expert"), None),
        P(),
        P(),
        P("dp"),
        P("dp"),
        P("dp", "expert", None, None),
    )
    out_specs = (P(("dp", "expert"), None), P("dp", "expert", None, None))
    return jax.shard_map(body, mesh=mesh, in_specs=in_specs, out_specs=out_specs, check_vma=False)
```

time: 73.7 us -> 62.7 us (0.85)
  local copies, waits for them, and re-layouts: 7.68 us -> 0.01 us
  Pallas kernels: 65.1 us -> 61.9 us
    unnamed x16 -> x6, local copies, waits for them, and re-layouts: 7.68 us -> 0.01 us
    pallas_call x1, Pallas kernels: 4.69 us -> 2.93 us  [body(): pl.pallas_call(settle, out_shape=(jax.ShapeDtypeStruct((SEG, width), bf16...]
    pallas_call x1, Pallas kernels: 60.4 us -> 59 us  [body(): pl.pallas_call(exchange, out_shape=(jax.ShapeDtypeStruct((SEG, width), bf...]
where the time goes in v2:
time: 62.7 us; the launch traced here: 62.6 us
  Pallas kernels  61.9 us (99%)
  between operations  0.69 us (1%)
    pallas_call x1, Pallas kernels, body(): pl.pallas_call(exchange, out_shape=(jax.ShapeDtypeStruct((SEG, width), bf...  59 us
    pallas_call x1, Pallas kernels, body(): pl.pallas_call(settle, out_shape=(jax.ShapeDtypeStruct((SEG, width), bf16...  2.93 us

profile of v2, /device:TPU:1, one launch (start us, length us, event | category | flops | bytes accessed | tf_op | source)
XLA Modules:
  0.0 62.6 jit_solution(14916297841785108217)
XLA Ops:
  0.6 0.0 copy-start
  0.6 0.0 copy-start.1
  0.7 0.0 copy-start.2
  0.7 59.0 %exchange.1 = (bf16[256,4096]{1,0:T(8,128)(2,1)S(1)}, bf16[16,2,128,128]{3,2,1,0:T(8,128)(2,1)S(1)}, bf16[16,2,128,128]{3,2,1,0:T(8,128)(2,1)S(1)}) custom-call(bf16[256,4096]{1,0:T(8,128)(2,1)} %q_hbm.1, bf16[256,4096]{1,0:T(8,128)(2,1)} %k_hbm.1, bf16[256,4096]{1,0:T(8,128)(2,1)} %v_hbm.1, f32[32]{0:T(128)} %slopes.1, s32[16]{0:T(128)} %parents_hbm.1, ...), custom_call_target="tpu_custom_call" | custom-call | tf_op jit(solution)/shard_map/exchange/pallas_call | solution.py:302
  59.7 0.0 copy-done
  59.7 0.0 copy-done.1
  59.7 0.0 copy-done.2
  59.7 2.9 %settle.1 = (bf16[256,4096]{1,0:T(8,128)(2,1)}, f32[16,2,128,128]{3,2,1,0:T(8,128)}) custom-call(bf16[256,4096]{1,0:T(8,128)(2,1)S(1)} %get-tuple-element.5.att, bf16[16,2,128,128]{3,2,1,0:T(8,128)(2,1)S(1)} %get-tuple-element.6.got_u, bf16[16,2,128,128]{3,2,1,0:T(8,128)(2,1)S(1)} %get-tuple-element.7.start, f32[1,4096]{1,0:T(1,128)S(1)} %bitcast.1, ...), custom_call_target="tpu_custom_call" | custom-call | tf_op jit(solution)/shard_map/settle/pallas_call | solution.py:340
Async XLA Ops:
  0.6 59.0 %copy-start = (f32[4096]{0:T(1024)S(1)}, f32[4096]{0:T(1024)}, u32[]{:S(2)}) copy-start(f32[4096]{0:T(1024)} %param.12) | copy-start | bytes 49156
  0.6 59.0 %copy-start.1 = (f32[32]{0:T(128)S(1)}, f32[32]{0:T(128)}, u32[]{:S(2)}) copy-start(f32[32]{0:T(128)} %slopes.1) | copy-start | bytes 388
  0.7 59.0 %copy-start.2 = (s32[16]{0:T(128)S(1)}, s32[16]{0:T(128)}, u32[]{:S(2)}) copy-start(s32[16]{0:T(128)} %lengths.1) | copy-start | bytes 196

commit v3 on v2

v3 whole, which is shorter than its diff:
```python
import jax
import jax.numpy as jnp
from jax import lax
from jax.experimental import pallas as pl
from jax.experimental.pallas import tpu as pltpu
from jax.sharding import PartitionSpec as P

EPS = 1e-06
MESH = pl.DeviceIdType.MESH
SIDE = 4
RING = 8
GROUP = 16
HEADS = 32
DIM = 128
SEG = 256
PAIR = 2 * DIM
CUTS = 4
FAR = 1e9
EARLY, MIDDLE = 10, 22


def ring_step(i):
    j = i // 2
    off = RING // 2 + ((j + 1) // 2) * (1 - 2 * (j % 2))
    return off, (i + 1) % 2


def exchange(
    q_hbm, k_hbm, v_hbm, slopes_hbm, parents_hbm, lengths_hbm, states_hbm,
    att, child,
    q, k, v, slopes, parents, lengths, states, total, offsets, sent_u, got_u, bank_own, bank_far, picked, passed, got_s,
    load_sem, small_sem, swap_sem, bank_send, bank_hop, bank_recv, u_send, u_recv, s_send, p_send, s_recv,
):
    me_d = lax.axis_index("dp")
    me_e = lax.axis_index("expert")
    y, x = me_d // SIDE, me_d % SIDE
    z, core = me_e // 2, me_e % 2
    across = (me_e + GROUP // 2) % GROUP

    arrays = ((k_hbm, k), (v_hbm, v), (q_hbm, q))

    def load(n, cut):
        rows = pl.ds(cut * (SEG // CUTS), SEG // CUTS)
        src, dst = arrays[n]
        return pltpu.make_async_copy(src.at[rows], dst.at[rows], load_sem.at[n, cut])

    smalls = [
        pltpu.make_async_copy(src, dst, small_sem.at[n])
        for n, (src, dst) in enumerate(
            ((states_hbm, states), (slopes_hbm, slopes), (lengths_hbm, lengths), (parents_hbm, parents))
        )
    ]
    for small in smalls:
        small.start()
    for n in range(3):
        for cut in range(CUTS):
            load(n, cut).start()

    def along(slot, j):
        return y * SIDE + (x + j) % SIDE if slot % 2 == 0 else ((y + j) % SIDE) * SIDE + x

    barrier = pltpu.get_barrier_semaphore()

    def greet(i, _):
        pl.semaphore_signal(
            barrier, inc=1, device_id=(me_d, (me_e + i) % GROUP), device_id_type=MESH
        )
        return 0

    lax.fori_loop(1, GROUP, greet, 0)
    for slot in range(2):
        for j in range(1, SIDE):
            pl.semaphore_signal(
                barrier, inc=1, device_id=(along(slot, j), me_e), device_id_type=MESH
            )

    for small in smalls:
        small.wait()

    for slot in range(2):
        for parent in range(2):
            bank_own[slot, 2 * me_d + parent] = states[parent, slot].astype(jnp.bfloat16)

    t_of = lax.broadcasted_iota(jnp.int32, (SEG, SEG), 0)
    s_of = lax.broadcasted_iota(jnp.int32, (SEG, SEG), 1)
    offsets[...] = jnp.where(t_of >= s_of, (t_of - s_of).astype(jnp.float32), FAR)

    length = lengths[me_e]
    place = lax.broadcasted_iota(jnp.int32, (SEG, DIM), 0)
    remain = (length - 1 - place).astype(jnp.float32)
    inside = place < length
    step_of = (place + 1).astype(jnp.float32)

    def head_columns(e, head):
        return pl.ds(pl.multiple_of(e * PAIR + head * DIM, DIM), DIM)

    def device(off, flip):
        return 2 * ((z + off) % RING) + (core + flip) % 2

    def partner(i):
        return device(*ring_step(i))

    def source(i):
        off, flip = ring_step(i)
        return device(RING - off, flip)

    def near(far, i):
        return device(far + (RING - 2 * far) * (i // 2), i % 2)

    other = device(0, 1)

    def update(e):
        for head in range(2):
            cols = head_columns(e, head)
            slope = slopes[2 * e + head]
            fade = jnp.where(remain >= 0.0, jnp.exp(-slope * jnp.maximum(remain, 0.0)), 0.0)
            keys = (k[:, cols].astype(jnp.float32) * fade).astype(jnp.bfloat16)
            sent_u[e, head] = lax.dot_general(
                keys, v[:, cols], (((0,), (0,)), ((), ())), preferred_element_type=jnp.float32
            ).astype(jnp.bfloat16)

    for cut in range(CUTS):
        load(0, cut).wait()
        load(1, cut).wait()
    update(partner(0))

    pl.semaphore_wait(barrier, GROUP - 1 + 2 * (SIDE - 1))

    swap = pltpu.make_async_remote_copy(
        src_ref=bank_own.at[:, pl.ds(2 * me_d, 2)],
        dst_ref=bank_far.at[:, pl.ds(2 * me_d, 2)],
        send_sem=swap_sem.at[0], recv_sem=swap_sem.at[1],
        device_id=(me_d, across), device_id_type=MESH,
    )
    swap.start()

    def bank_copy(slot, d, to, sem):
        block = (bank_own, bank_far)[slot // 2].at[slot % 2, pl.ds(2 * d, 2)]
        return pltpu.make_async_remote_copy(
            src_ref=block, dst_ref=block, send_sem=sem,
            recv_sem=bank_recv.at[slot, d], device_id=(to, me_e), device_id_type=MESH,
        )

    def first_hop(slot, j):
        return bank_copy(slot, me_d, along(slot, j), bank_send.at[slot, j - 1])

    def second_hop(slot, b, j):
        return bank_copy(slot, along(slot, b), along(slot + 1, j), bank_hop.at[slot, b, j - 1])

    def arrival(slot, d):
        bank_copy(slot, d, along(0, 1), bank_send.at[slot, 0]).wait_recv()

    def open_gather(slots):
        for slot in slots:
            for j in range(1, SIDE):
                first_hop(slot, j).start()
        for slot in slots:
            for j in range(1, SIDE):
                second_hop(slot, 0, j).start()

    def pass_on(slots):
        for b in range(1, SIDE):
            for slot in slots:
                arrival(slot, along(slot, b))
                for j in range(1, SIDE):
                    second_hop(slot, b, j).start()

    def close_gather(slots):
        for j in range(1, SIDE):
            for b in range(SIDE):
                for slot in slots:
                    if slot % 2 == 0:
                        arrival(slot, ((y + j) % SIDE) * SIDE + (x + b) % SIDE)
                    else:
                        arrival(slot, ((y + b) % SIDE) * SIDE + (x + j) % SIDE)

    open_gather((0, 1))

    def send_u(e):
        return pltpu.make_async_remote_copy(
            src_ref=sent_u.at[e], dst_ref=got_u.at[me_e], send_sem=u_send.at[e],
            recv_sem=u_recv.at[me_e], device_id=(me_d, e), device_id_type=MESH,
        )

    def recv_u(e):
        return pltpu.make_async_remote_copy(
            src_ref=sent_u.at[e], dst_ref=got_u.at[e], send_sem=u_send.at[e],
            recv_sem=u_recv.at[e], device_id=(me_d, e), device_id_type=MESH,
        )

    def send_s(e):
        return pltpu.make_async_remote_copy(
            src_ref=picked.at[e], dst_ref=got_s.at[me_e], send_sem=s_send.at[e],
            recv_sem=s_recv.at[me_e], device_id=(me_d, e), device_id_type=MESH,
        )

    def send_p(e):
        return pltpu.make_async_remote_copy(
            src_ref=passed.at[e], dst_ref=got_s.at[across], send_sem=p_send.at[e],
            recv_sem=s_recv.at[across], device_id=(me_d, e), device_id_type=MESH,
        )

    def recv_s(e):
        return pltpu.make_async_remote_copy(
            src_ref=picked.at[e], dst_ref=got_s.at[e], send_sem=s_send.at[e],
            recv_sem=s_recv.at[e], device_id=(me_d, e), device_id_type=MESH,
        )

    def update_step(i, _):
        send_u(partner(i)).start()
        update(partner(i + 1))
        return 0

    lax.fori_loop(0, GROUP - 1, update_step, 0)

    pass_on((0, 1))
    swap.wait_recv()
    open_gather((2, 3))

    for cut in range(CUTS):
        load(2, cut).wait()

    def within(i, _):
        cols = pl.ds(pl.multiple_of(i * DIM, DIM), DIM)
        decay = jnp.exp(-slopes[i] * offsets[...])
        scores = lax.dot_general(
            q[:, cols], k[:, cols], (((1,), (1,)), ((), ())), preferred_element_type=jnp.float32
        )
        total[:, cols] = jnp.dot(
            (scores * decay).astype(jnp.bfloat16), v[:, cols], preferred_element_type=jnp.float32
        )
        return 0

    lax.fori_loop(0, EARLY, within, 0)
    pass_on((2, 3))
    lax.fori_loop(EARLY, MIDDLE, within, 0)

    def pick(e, bank, into):
        parent = parents[e]
        for head in range(2):
            into[e, head] = bank[head, parent]

    def pick_far(i, _):
        e = near(2, i)
        pick(e, bank_own, picked)
        send_s(e).start()
        return 0

    def pick_next(i, _):
        e = near(1, i)
        pick(e, bank_own, picked)
        send_s(e).start()
        return 0

    def pick_rest(i, _):
        off = 3 + i // 2
        pick(device(off, i % 2), bank_own, picked)
        return 0

    close_gather((0, 1))
    lax.fori_loop(0, 4, pick_far, 0)
    lax.fori_loop(0, 4, pick_next, 0)
    pick(other, bank_own, picked)
    send_s(other).start()
    pick(me_e, bank_own, picked)
    lax.fori_loop(0, 6, pick_rest, 0)

    lax.fori_loop(MIDDLE, HEADS, within, 0)

    def grow(e, fresh):
        for head in range(2):
            fade = jnp.exp(
                jnp.full((1, DIM), -slopes[2 * me_e + head] * lengths[e].astype(jnp.float32), jnp.float32)
            )
            child[e, head] = fade * picked[e, head].astype(jnp.float32) + fresh[e, head].astype(
                jnp.float32
            )

    def grow_step(i, _):
        e = source(i)
        recv_u(e).wait_recv()
        grow(e, got_u)
        return 0

    grow(me_e, sent_u)
    lax.fori_loop(0, GROUP - 1, grow_step, 0)

    def pass_next(i, _):
        e = near(1, i)
        pick(e, bank_far, passed)
        send_p(e).start()
        return 0

    close_gather((2, 3))
    lax.fori_loop(0, 4, pass_next, 0)
    pick(other, bank_far, passed)
    send_p(other).start()
    pick(me_e, bank_far, passed)

    def finish(e, src, at):
        for head in range(2):
            cols = head_columns(e, head)
            lead = jnp.exp(-slopes[2 * e + head] * step_of)
            carried = jnp.dot(q[:, cols], src[at, head], preferred_element_type=jnp.float32)
            att[:, cols] = jnp.where(inside, total[:, cols] + carried * lead, 0.0).astype(jnp.bfloat16)

    def arrived(e):
        recv_s(e).wait_recv()
        finish(e, got_s, e)

    def finish_far(i, _):
        arrived(near(2, i))
        return 0

    def finish_next(i, _):
        arrived(near(1, i))
        return 0

    def finish_passed(i, _):
        arrived((near(1, i) + GROUP // 2) % GROUP)
        return 0

    finish(me_e, picked, me_e)
    finish(across, passed, me_e)
    arrived(other)
    lax.fori_loop(0, 4, finish_far, 0)
    lax.fori_loop(0, 4, finish_next, 0)
    arrived((other + GROUP // 2) % GROUP)
    lax.fori_loop(0, 4, finish_passed, 0)

    def drain_u(i, _):
        send_u(partner(i)).wait_send()
        return 0

    def drain_s(i, _):
        send_s(near(2, i)).wait_send()
        send_s(near(1, i)).wait_send()
        send_p(near(1, i)).wait_send()
        return 0

    lax.fori_loop(0, GROUP - 1, drain_u, 0)
    lax.fori_loop(0, 4, drain_s, 0)
    send_s(other).wait_send()
    send_p(other).wait_send()
    swap.wait_send()
    for slot in range(4):
        for j in range(1, SIDE):
            first_hop(slot, j).wait_send()
            for b in range(SIDE):
                second_hop(slot, b, j).wait_send()


STEPS = 8
TOKENS = SEG // STEPS


def settle(att, child, gain, mixed_hbm, child_hbm, mixed, child_sem, mixed_sem):
    kids = GROUP // STEPS

    def child_out(at):
        part = pl.ds(at * kids, kids)
        return pltpu.make_async_copy(child.at[part], child_hbm.at[part], child_sem.at[at])

    def mixed_out(at):
        part = pl.ds(at * TOKENS, TOKENS)
        return pltpu.make_async_copy(mixed.at[part], mixed_hbm.at[part], mixed_sem.at[at])

    def step(at, _):
        here = pl.ds(pl.multiple_of(at * TOKENS, TOKENS), TOKENS)
        rows = att[here, :].astype(jnp.float32)
        mean = jnp.mean(rows * rows, axis=-1, keepdims=True)
        mixed[here, :] = (rows * lax.rsqrt(mean + EPS) * gain[...]).astype(jnp.bfloat16)
        mixed_out(at).start()
        return 0

    for at in range(STEPS):
        child_out(at).start()
    lax.fori_loop(0, STEPS, step, 0)
    for at in range(STEPS):
        child_out(at).wait()
        mixed_out(at).wait()


def body(queries, key_rows, value_rows, slopes, norm_gain, parents, lengths, parent_states):
    anywhere = pl.BlockSpec(memory_space=pl.ANY)
    vmem = pl.BlockSpec(memory_space=pltpu.VMEM)
    dma = pltpu.SemaphoreType.DMA
    bf16, f32 = jnp.bfloat16, jnp.float32
    width = HEADS * DIM
    moved = (GROUP, 2, DIM, DIM)
    in_hbm = [
        pltpu.with_memory_space_constraint(a, pltpu.HBM)
        for a in (queries, key_rows, value_rows, slopes, parents, lengths, parent_states)
    ]
    att, child = pl.pallas_call(
        exchange,
        out_shape=(
            jax.ShapeDtypeStruct((SEG, width), bf16),
            jax.ShapeDtypeStruct(moved, f32),
        ),
        in_specs=[anywhere] * 7,
        out_specs=(vmem,) * 2,
        scratch_shapes=[
            pltpu.VMEM((SEG, width), bf16),
            pltpu.VMEM((SEG, width), bf16),
            pltpu.VMEM((SEG, width), bf16),
            pltpu.SMEM((HEADS,), f32),
            pltpu.SMEM((GROUP,), jnp.int32),
            pltpu.SMEM((GROUP,), jnp.int32),
            pltpu.VMEM((2, 2, DIM, DIM), f32),
            pltpu.VMEM((SEG, width), f32),
            pltpu.VMEM((SEG, SEG), f32),
            pltpu.VMEM(moved, bf16),
            pltpu.VMEM(moved, bf16),
            pltpu.VMEM((2, 2 * SIDE * SIDE, DIM, DIM), bf16),
            pltpu.VMEM((2, 2 * SIDE * SIDE, DIM, DIM), bf16),
            pltpu.VMEM(moved, bf16),
            pltpu.VMEM(moved, bf16),
            pltpu.VMEM(moved, bf16),
            dma((3, CUTS)),
            dma((4,)),
            dma((2,)),
            dma((4, SIDE - 1)),
            dma((4, SIDE, SIDE - 1)),
            dma((4, SIDE * SIDE)),
            dma((GROUP,)),
            dma((GROUP,)),
            dma((GROUP,)),
            dma((GROUP,)),
            dma((GROUP,)),
        ],
        compiler_params=pltpu.CompilerParams(
            collective_id=0, has_side_effects=True, vmem_limit_bytes=40 * 1024 * 1024
        ),
        name="exchange",
    )(*in_hbm)
    mixed, child = pl.pallas_call(
        settle,
        out_shape=(
            jax.ShapeDtypeStruct((SEG, width), bf16),
            jax.ShapeDtypeStruct(moved, f32),
        ),
        in_specs=[vmem] * 3,
        out_specs=(anywhere,) * 2,
        scratch_shapes=[
            pltpu.VMEM((SEG, width), bf16),
            dma((STEPS,)),
            dma((STEPS,)),
        ],
        compiler_params=pltpu.CompilerParams(vmem_limit_bytes=32 * 1024 * 1024),
        name="settle",
    )(att, child, norm_gain.reshape(1, width))
    return mixed, child


def solution(mesh):
    in_specs = (
        P(("dp", "expert"), None),
        P(("dp", "expert"), None),
        P(("dp", "expert"), None),
        P(),
        P(),
        P("dp"),
        P("dp"),
        P("dp", "expert", None, None),
    )
    out_specs = (P(("dp", "expert"), None), P("dp", "expert", None, None))
    return jax.shard_map(body, mesh=mesh, in_specs=in_specs, out_specs=out_specs, check_vma=False)
```

time: 62.7 us -> 56.5 us (0.901)
  Pallas kernels: 61.9 us -> 55.8 us
    pallas_call x1, Pallas kernels: 59 us -> 53.6 us  [body(): pl.pallas_call(exchange, out_shape=(jax.ShapeDtypeStruct((SEG, width), bf...]
    pallas_call x1, Pallas kernels: 2.93 us -> 2.24 us  [body(): pl.pallas_call(settle, out_shape=(jax.ShapeDtypeStruct((SEG, width), bf16...]
where the time goes in v3:
time: 56.5 us
  Pallas kernels  55.8 us (99%)
  between operations  0.66 us (1%)
    pallas_call x1, Pallas kernels, body(): pl.pallas_call(exchange, out_shape=(jax.ShapeDtypeStruct((SEG, width), bf...  53.6 us
    pallas_call x1, Pallas kernels, body(): pl.pallas_call(settle, out_shape=(jax.ShapeDtypeStruct((SEG, width), bf16...  2.24 us

profile of v3, /device:TPU:1, one launch (start us, length us, event | category | flops | bytes accessed | tf_op | source)
XLA Modules:
  0.0 56.5 jit_solution(3305683131815861782)
XLA Ops:
  0.6 0.0 copy-start
  0.6 53.6 %exchange.1 = (bf16[256,4096]{1,0:T(8,128)(2,1)S(1)}, f32[16,2,128,128]{3,2,1,0:T(8,128)S(1)}) custom-call(bf16[256,4096]{1,0:T(8,128)(2,1)} %q_hbm.1, bf16[256,4096]{1,0:T(8,128)(2,1)} %k_hbm.1, bf16[256,4096]{1,0:T(8,128)(2,1)} %v_hbm.1, f32[32]{0:T(128)} %slopes_hbm.1, s32[16]{0:T(128)} %parents_hbm.1, s32[16]{0:T(128)} %lengths_hbm.1, ...), custom_call_target="tpu_custom_call" | custom-call | tf_op jit(solution)/shard_map/exchange/pallas_call | solution.py:395
  54.2 0.0 copy-done
  54.2 2.2 %settle.1 = (bf16[256,4096]{1,0:T(8,128)(2,1)}, f32[16,2,128,128]{3,2,1,0:T(8,128)}) custom-call(bf16[256,4096]{1,0:T(8,128)(2,1)S(1)} %get-tuple-element.4.att, f32[16,2,128,128]{3,2,1,0:T(8,128)S(1)} %get-tuple-element.5.child, f32[1,4096]{1,0:T(1,128)S(1)} %bitcast.1), custom_call_target="tpu_custom_call" | custom-call | tf_op jit(solution)/shard_map/settle/pallas_call | solution.py:437
Async XLA Ops:
  0.6 53.6 %copy-start = (f32[4096]{0:T(1024)S(1)}, f32[4096]{0:T(1024)}, u32[]{:S(2)}) copy-start(f32[4096]{0:T(1024)} %param.12) | copy-start | bytes 49156

commit v4 on v3

v4 whole, which is shorter than its diff:
```python
import jax
import jax.numpy as jnp
from jax import lax
from jax.experimental import pallas as pl
from jax.experimental.pallas import tpu as pltpu
from jax.sharding import PartitionSpec as P

EPS = 1e-06
MESH = pl.DeviceIdType.MESH
SIDE = 4
RING = 8
GROUP = 16
HEADS = 32
DIM = 128
SEG = 256
PAIR = 2 * DIM
CUTS = 4
FAR = 1e9
SWAP = 3
EARLY, MIDDLE = 10, 22


def ring_step(i):
    j = i // 2
    off = RING // 2 + ((j + 1) // 2) * (1 - 2 * (j % 2))
    return off, (i + 1) % 2


def exchange(
    q_hbm, k_hbm, v_hbm, slopes_hbm, parents_hbm, lengths_hbm, states_hbm,
    att, child,
    q, k, v, slopes, parents, lengths, states, total, offsets, sent_u, got_u, bank_own, bank_far, picked, passed, got_s,
    load_sem, small_sem, swap_sem, bank_send, bank_hop, bank_recv, u_send, u_recv, s_send, p_send, s_recv,
):
    me_d = lax.axis_index("dp")
    me_e = lax.axis_index("expert")
    y, x = me_d // SIDE, me_d % SIDE
    z, core = me_e // 2, me_e % 2

    arrays = ((k_hbm, k), (v_hbm, v), (q_hbm, q))

    def load(n, cut):
        rows = pl.ds(cut * (SEG // CUTS), SEG // CUTS)
        src, dst = arrays[n]
        return pltpu.make_async_copy(src.at[rows], dst.at[rows], load_sem.at[n, cut])

    def along(slot, j):
        return y * SIDE + (x + j) % SIDE if slot % 2 == 0 else ((y + j) % SIDE) * SIDE + x

    barrier = pltpu.get_barrier_semaphore()

    def greet(i, _):
        pl.semaphore_signal(
            barrier, inc=1, device_id=(me_d, (me_e + i) % GROUP), device_id_type=MESH
        )
        return 0

    lax.fori_loop(1, GROUP, greet, 0)
    for slot in range(2):
        for j in range(1, SIDE):
            pl.semaphore_signal(
                barrier, inc=1, device_id=(along(slot, j), me_e), device_id_type=MESH
            )

    smalls = [
        pltpu.make_async_copy(src, dst, small_sem.at[n])
        for n, (src, dst) in enumerate(
            ((states_hbm, states), (slopes_hbm, slopes), (lengths_hbm, lengths), (parents_hbm, parents))
        )
    ]
    for small in smalls:
        small.start()
    for n in range(3):
        for cut in range(CUTS):
            load(n, cut).start()

    smalls[0].wait()

    for slot in range(2):
        for parent in range(2):
            bank_own[slot, 2 * me_d + parent] = states[parent, slot].astype(jnp.bfloat16)

    def head_columns(e, head):
        return pl.ds(pl.multiple_of(e * PAIR + head * DIM, DIM), DIM)

    def device(off, flip):
        return 2 * ((z + off) % RING) + (core + flip) % 2

    def partner(i):
        return device(*ring_step(i))

    def source(i):
        off, flip = ring_step(i)
        return device(RING - off, flip)

    def giver(slot, i):
        n = i // 2
        up = 1 + 7 * n - 2 * n * n
        return device(up + slot * (RING - 2 * up), i % 2)

    def taker(slot, i):
        return giver(1 - slot, i)

    def kept_for(e, slot):
        return (e + 2 * SWAP + slot * (GROUP - 4 * SWAP)) % GROUP

    other = device(0, 1)

    pl.semaphore_wait(barrier, GROUP - 1 + 2 * (SIDE - 1))

    def swap(slot):
        return pltpu.make_async_remote_copy(
            src_ref=bank_own.at[slot, pl.ds(2 * me_d, 2)],
            dst_ref=bank_far.at[slot, pl.ds(2 * me_d, 2)],
            send_sem=swap_sem.at[0, slot], recv_sem=swap_sem.at[1, slot],
            device_id=(me_d, device(SWAP if slot else RING - SWAP, 0)), device_id_type=MESH,
        )

    swap(0).start()
    swap(1).start()

    def bank_copy(slot, d, to, sem):
        block = (bank_own, bank_far)[slot // 2].at[slot % 2, pl.ds(2 * d, 2)]
        return pltpu.make_async_remote_copy(
            src_ref=block, dst_ref=block, send_sem=sem,
            recv_sem=bank_recv.at[slot, d], device_id=(to, me_e), device_id_type=MESH,
        )

    def first_hop(slot, j):
        return bank_copy(slot, me_d, along(slot, j), bank_send.at[slot, j - 1])

    def second_hop(slot, b, j):
        return bank_copy(slot, along(slot, b), along(slot + 1, j), bank_hop.at[slot, b, j - 1])

    def arrival(slot, d):
        bank_copy(slot, d, along(0, 1), bank_send.at[slot, 0]).wait_recv()

    def open_gather(slots):
        for slot in slots:
            for j in range(1, SIDE):
                first_hop(slot, j).start()
        for slot in slots:
            for j in range(1, SIDE):
                second_hop(slot, 0, j).start()

    def pass_on(slots):
        for b in range(1, SIDE):
            for slot in slots:
                arrival(slot, along(slot, b))
                for j in range(1, SIDE):
                    second_hop(slot, b, j).start()

    def close_gather(slots):
        for j in range(1, SIDE):
            for b in range(SIDE):
                for slot in slots:
                    if slot % 2 == 0:
                        arrival(slot, ((y + j) % SIDE) * SIDE + (x + b) % SIDE)
                    else:
                        arrival(slot, ((y + b) % SIDE) * SIDE + (x + j) % SIDE)

    open_gather((0, 1))

    for small in smalls[1:]:
        small.wait()

    length = lengths[me_e]
    place = lax.broadcasted_iota(jnp.int32, (SEG, DIM), 0)
    remain = (length - 1 - place).astype(jnp.float32)
    inside = place < length
    step_of = (place + 1).astype(jnp.float32)

    def update(e):
        for head in range(2):
            cols = head_columns(e, head)
            slope = slopes[2 * e + head]
            fade = jnp.where(remain >= 0.0, jnp.exp(-slope * jnp.maximum(remain, 0.0)), 0.0)
            keys = (k[:, cols].astype(jnp.float32) * fade).astype(jnp.bfloat16)
            sent_u[e, head] = lax.dot_general(
                keys, v[:, cols], (((0,), (0,)), ((), ())), preferred_element_type=jnp.float32
            ).astype(jnp.bfloat16)

    for cut in range(CUTS):
        load(0, cut).wait()
        load(1, cut).wait()
    update(partner(0))

    def send_u(e):
        return pltpu.make_async_remote_copy(
            src_ref=sent_u.at[e], dst_ref=got_u.at[me_e], send_sem=u_send.at[e],
            recv_sem=u_recv.at[me_e], device_id=(me_d, e), device_id_type=MESH,
        )

    def recv_u(e):
        return pltpu.make_async_remote_copy(
            src_ref=sent_u.at[e], dst_ref=got_u.at[e], send_sem=u_send.at[e],
            recv_sem=u_recv.at[e], device_id=(me_d, e), device_id_type=MESH,
        )

    def send_own(e, slot):
        return pltpu.make_async_remote_copy(
            src_ref=picked.at[e, slot], dst_ref=got_s.at[me_e, slot], send_sem=s_send.at[e, slot],
            recv_sem=s_recv.at[me_e, slot], device_id=(me_d, e), device_id_type=MESH,
        )

    def send_far(e, slot):
        owner = kept_for(me_e, slot)
        return pltpu.make_async_remote_copy(
            src_ref=passed.at[e, slot], dst_ref=got_s.at[owner, slot], send_sem=p_send.at[e, slot],
            recv_sem=s_recv.at[owner, slot], device_id=(me_d, e), device_id_type=MESH,
        )

    def recv_s(e, slot):
        return pltpu.make_async_remote_copy(
            src_ref=picked.at[e, slot], dst_ref=got_s.at[e, slot], send_sem=s_send.at[e, slot],
            recv_sem=s_recv.at[e, slot], device_id=(me_d, e), device_id_type=MESH,
        )

    def update_step(i, _):
        send_u(partner(i)).start()
        update(partner(i + 1))
        return 0

    lax.fori_loop(0, GROUP - 1, update_step, 0)

    pass_on((0, 1))
    swap(0).wait_recv()
    swap(1).wait_recv()
    open_gather((2, 3))

    t_of = lax.broadcasted_iota(jnp.int32, (SEG, SEG), 0)
    s_of = lax.broadcasted_iota(jnp.int32, (SEG, SEG), 1)
    offsets[...] = jnp.where(t_of >= s_of, (t_of - s_of).astype(jnp.float32), FAR)

    for cut in range(CUTS):
        load(2, cut).wait()

    def within(i, _):
        cols = pl.ds(pl.multiple_of(i * DIM, DIM), DIM)
        decay = jnp.exp(-slopes[i] * offsets[...])
        scores = lax.dot_general(
            q[:, cols], k[:, cols], (((1,), (1,)), ((), ())), preferred_element_type=jnp.float32
        )
        total[:, cols] = jnp.dot(
            (scores * decay).astype(jnp.bfloat16), v[:, cols], preferred_element_type=jnp.float32
        )
        return 0

    lax.fori_loop(0, EARLY, within, 0)
    pass_on((2, 3))
    lax.fori_loop(EARLY, MIDDLE, within, 0)

    def pick(e, _):
        parent = parents[e]
        for slot in range(2):
            picked[e, slot] = bank_own[slot, parent]
        return 0

    def each_other(step):
        def both(i, _):
            for slot in range(2):
                step(slot, i)
            return 0

        lax.fori_loop(0, 6, both, 0)

    close_gather((0, 1))
    lax.fori_loop(0, GROUP, pick, 0)
    each_other(lambda slot, i: send_own(taker(slot, i), slot).start())
    for slot in range(2):
        send_own(other, slot).start()

    lax.fori_loop(MIDDLE, HEADS, within, 0)

    def grow(e, fresh):
        for head in range(2):
            fade = jnp.exp(
                jnp.full((1, DIM), -slopes[2 * me_e + head] * lengths[e].astype(jnp.float32), jnp.float32)
            )
            child[e, head] = fade * picked[e, head].astype(jnp.float32) + fresh[e, head].astype(
                jnp.float32
            )

    def grow_step(i, _):
        e = source(i)
        recv_u(e).wait_recv()
        send_u(partner(i)).wait_send()
        grow(e, got_u)
        return 0

    def select(e, slot):
        passed[e, slot] = bank_far[slot, parents[e]]

    def pass_far(slot, i):
        e = giver(slot, i)
        select(e, slot)
        send_far(e, slot).start()

    close_gather((2, 3))
    each_other(pass_far)
    for slot in range(2):
        select(other, slot)
        send_far(other, slot).start()
        select(me_e, slot)

    def finish(owner, slot, src, at):
        cols = head_columns(owner, slot)
        lead = jnp.exp(-slopes[2 * owner + slot] * step_of)
        carried = jnp.dot(q[:, cols], src[at, slot], preferred_element_type=jnp.float32)
        att[:, cols] = jnp.where(inside, total[:, cols] + carried * lead, 0.0).astype(jnp.bfloat16)

    def arrived(owner, slot):
        recv_s(owner, slot).wait_recv()
        finish(owner, slot, got_s, owner)

    def finish_here(slot, _):
        finish(me_e, slot, picked, me_e)
        finish(kept_for(me_e, slot), slot, passed, me_e)
        return 0

    def finish_other(slot, _):
        send_own(other, slot).wait_send()
        send_far(other, slot).wait_send()
        arrived(other, slot)
        arrived(kept_for(other, slot), slot)
        return 0

    def finish_own(j, _):
        i, slot = j // 2, j % 2
        arrived(giver(slot, i), slot)
        send_own(taker(slot, i), slot).wait_send()
        return 0

    def finish_far(j, _):
        i, slot = j // 2, j % 2
        arrived(kept_for(taker(slot, i), slot), slot)
        send_far(giver(slot, i), slot).wait_send()
        return 0

    lax.fori_loop(0, 2, finish_here, 0)
    swap(0).wait_send()
    swap(1).wait_send()
    for slot in range(4):
        for j in range(1, SIDE):
            first_hop(slot, j).wait_send()
            for b in range(SIDE):
                second_hop(slot, b, j).wait_send()
    grow(me_e, sent_u)
    lax.fori_loop(0, GROUP - 1, grow_step, 0)
    lax.fori_loop(0, 2, finish_other, 0)
    lax.fori_loop(0, 12, finish_own, 0)
    lax.fori_loop(0, 12, finish_far, 0)


STEPS = 4
TOKENS = SEG // STEPS


def settle(att, child, gain, mixed_hbm, child_hbm, mixed, child_sem, mixed_sem):
    kids = GROUP // STEPS

    def child_out(at):
        part = pl.ds(at * kids, kids)
        return pltpu.make_async_copy(child.at[part], child_hbm.at[part], child_sem.at[at])

    def mixed_out(at):
        part = pl.ds(at * TOKENS, TOKENS)
        return pltpu.make_async_copy(mixed.at[part], mixed_hbm.at[part], mixed_sem.at[at])

    def step(at, _):
        here = pl.ds(pl.multiple_of(at * TOKENS, TOKENS), TOKENS)
        rows = att[here, :].astype(jnp.float32)
        mean = jnp.mean(rows * rows, axis=-1, keepdims=True)
        mixed[here, :] = (rows * lax.rsqrt(mean + EPS) * gain[...]).astype(jnp.bfloat16)
        mixed_out(at).start()
        return 0

    for at in range(STEPS):
        child_out(at).start()
    lax.fori_loop(0, STEPS, step, 0)
    for at in range(STEPS):
        child_out(at).wait()
        mixed_out(at).wait()


def body(queries, key_rows, value_rows, slopes, norm_gain, parents, lengths, parent_states):
    anywhere = pl.BlockSpec(memory_space=pl.ANY)
    vmem = pl.BlockSpec(memory_space=pltpu.VMEM)
    dma = pltpu.SemaphoreType.DMA
    bf16, f32 = jnp.bfloat16, jnp.float32
    width = HEADS * DIM
    moved = (GROUP, 2, DIM, DIM)
    in_hbm = [
        pltpu.with_memory_space_constraint(a, pltpu.HBM)
        for a in (queries, key_rows, value_rows, slopes, parents, lengths, parent_states)
    ]
    att, child = pl.pallas_call(
        exchange,
        out_shape=(
            jax.ShapeDtypeStruct((SEG, width), bf16),
            jax.ShapeDtypeStruct(moved, f32),
        ),
        in_specs=[anywhere] * 7,
        out_specs=(vmem,) * 2,
        scratch_shapes=[
            pltpu.VMEM((SEG, width), bf16),
            pltpu.VMEM((SEG, width), bf16),
            pltpu.VMEM((SEG, width), bf16),
            pltpu.SMEM((HEADS,), f32),
            pltpu.SMEM((GROUP,), jnp.int32),
            pltpu.SMEM((GROUP,), jnp.int32),
            pltpu.VMEM((2, 2, DIM, DIM), f32),
            pltpu.VMEM((SEG, width), f32),
            pltpu.VMEM((SEG, SEG), f32),
            pltpu.VMEM(moved, bf16),
            pltpu.VMEM(moved, bf16),
            pltpu.VMEM((2, 2 * SIDE * SIDE, DIM, DIM), bf16),
            pltpu.VMEM((2, 2 * SIDE * SIDE, DIM, DIM), bf16),
            pltpu.VMEM(moved, bf16),
            pltpu.VMEM(moved, bf16),
            pltpu.VMEM(moved, bf16),
            dma((3, CUTS)),
            dma((4,)),
            dma((2, 2)),
            dma((4, SIDE - 1)),
            dma((4, SIDE, SIDE - 1)),
            dma((4, SIDE * SIDE)),
            dma((GROUP,)),
            dma((GROUP,)),
            dma((GROUP, 2)),
            dma((GROUP, 2)),
            dma((GROUP, 2)),
        ],
        compiler_params=pltpu.CompilerParams(
            collective_id=0, has_side_effects=True, vmem_limit_bytes=40 * 1024 * 1024
        ),
        name="exchange",
    )(*in_hbm)
    mixed, child = pl.pallas_call(
        settle,
        out_shape=(
            jax.ShapeDtypeStruct((SEG, width), bf16),
            jax.ShapeDtypeStruct(moved, f32),
        ),
        in_specs=[vmem] * 3,
        out_specs=(anywhere,) * 2,
        scratch_shapes=[
            pltpu.VMEM((SEG, width), bf16),
            dma((STEPS,)),
            dma((STEPS,)),
        ],
        compiler_params=pltpu.CompilerParams(vmem_limit_bytes=32 * 1024 * 1024),
        name="settle",
    )(att, child, norm_gain.reshape(1, width))
    return mixed, child


def solution(mesh):
    in_specs = (
        P(("dp", "expert"), None),
        P(("dp", "expert"), None),
        P(("dp", "expert"), None),
        P(),
        P(),
        P("dp"),
        P("dp"),
        P("dp", "expert", None, None),
    )
    out_specs = (P(("dp", "expert"), None), P("dp", "expert", None, None))
    return jax.shard_map(body, mesh=mesh, in_specs=in_specs, out_specs=out_specs, check_vma=False)
```

time: 56.5 us -> 54.5 us (0.965)
  Pallas kernels: 55.8 us -> 53.7 us
    pallas_call x1, Pallas kernels: 53.6 us -> 51.7 us  [body(): pl.pallas_call(exchange, out_shape=(jax.ShapeDtypeStruct((SEG, width), bf...]
where the time goes in v4:
time: 54.5 us; the launch traced here: 54.4 us
  Pallas kernels  53.7 us (99%)
  between operations  0.66 us (1%)
    pallas_call x1, Pallas kernels, body(): pl.pallas_call(exchange, out_shape=(jax.ShapeDtypeStruct((SEG, width), bf...  51.7 us
    pallas_call x1, Pallas kernels, body(): pl.pallas_call(settle, out_shape=(jax.ShapeDtypeStruct((SEG, width), bf16...  2.07 us

profile of v4, /device:TPU:1, one launch (start us, length us, event | category | flops | bytes accessed | tf_op | source)
XLA Modules:
  0.0 54.4 jit_solution(853268425430949593)
XLA Ops:
  0.6 0.0 copy-start
  0.6 51.7 %exchange.1 = (bf16[256,4096]{1,0:T(8,128)(2,1)S(1)}, f32[16,2,128,128]{3,2,1,0:T(8,128)S(1)}) custom-call(bf16[256,4096]{1,0:T(8,128)(2,1)} %q_hbm.1, bf16[256,4096]{1,0:T(8,128)(2,1)} %k_hbm.1, bf16[256,4096]{1,0:T(8,128)(2,1)} %v_hbm.1, f32[32]{0:T(128)} %slopes_hbm.1, s32[16]{0:T(128)} %parents_hbm.1, s32[16]{0:T(128)} %lengths_hbm.1, ...), custom_call_target="tpu_custom_call" | custom-call | tf_op jit(solution)/shard_map/exchange/pallas_call | solution.py:397
  52.3 0.0 copy-done
  52.3 2.1 %settle.1 = (bf16[256,4096]{1,0:T(8,128)(2,1)}, f32[16,2,128,128]{3,2,1,0:T(8,128)}) custom-call(bf16[256,4096]{1,0:T(8,128)(2,1)S(1)} %get-tuple-element.4.att, f32[16,2,128,128]{3,2,1,0:T(8,128)S(1)} %get-tuple-element.5.child, f32[1,4096]{1,0:T(1,128)S(1)} %bitcast.1), custom_call_target="tpu_custom_call" | custom-call | tf_op jit(solution)/shard_map/settle/pallas_call | solution.py:439
Async XLA Ops:
  0.6 51.7 %copy-start = (f32[4096]{0:T(1024)S(1)}, f32[4096]{0:T(1024)}, u32[]{:S(2)}) copy-start(f32[4096]{0:T(1024)} %param.12) | copy-start | bytes 49156

commit v5 on v4

--- a/solution.py
+++ b/solution.py
@@ -17,6 +17,7 @@
 CUTS = 4
 FAR = 1e9
 SWAP = 3
+LAST = 6
 EARLY, MIDDLE = 10, 22
 
 
@@ -30,7 +31,7 @@
     q_hbm, k_hbm, v_hbm, slopes_hbm, parents_hbm, lengths_hbm, states_hbm,
     att, child,
     q, k, v, slopes, parents, lengths, states, total, offsets, sent_u, got_u, bank_own, bank_far, picked, passed, got_s,
-    load_sem, small_sem, swap_sem, bank_send, bank_hop, bank_recv, u_send, u_recv, s_send, p_send, s_recv,
+    load_sem, small_sem, bank_send, swap_recv, first_recv, second_recv, u_sem, s_send, s_recv,
 ):
     me_d = lax.axis_index("dp")
     me_e = lax.axis_index("expert")
@@ -42,7 +43,10 @@
     def load(n, cut):
         rows = pl.ds(cut * (SEG // CUTS), SEG // CUTS)
         src, dst = arrays[n]
-        return pltpu.make_async_copy(src.at[rows], dst.at[rows], load_sem.at[n, cut])
+        return pltpu.make_async_copy(src.at[rows], dst.at[rows], load_sem.at[n])
+
+    def loaded(n):
+        pltpu.make_async_copy(*arrays[n], load_sem.at[n]).wait()
 
     def along(slot, j):
         return y * SIDE + (x + j) % SIDE if slot % 2 == 0 else ((y + j) % SIDE) * SIDE + x
@@ -112,28 +116,33 @@
         return pltpu.make_async_remote_copy(
             src_ref=bank_own.at[slot, pl.ds(2 * me_d, 2)],
             dst_ref=bank_far.at[slot, pl.ds(2 * me_d, 2)],
-            send_sem=swap_sem.at[0, slot], recv_sem=swap_sem.at[1, slot],
+            send_sem=bank_send.at[0], recv_sem=swap_recv.at[0],
             device_id=(me_d, device(SWAP if slot else RING - SWAP, 0)), device_id_type=MESH,
+        )
+
+    def batch(ref, sem):
+        return pltpu.make_async_remote_copy(
+            src_ref=ref, dst_ref=ref, send_sem=sem, recv_sem=sem,
+            device_id=(me_d, other), device_id_type=MESH,
         )
 
     swap(0).start()
     swap(1).start()
 
+    banks = (bank_own, bank_far)
+
     def bank_copy(slot, d, to, sem):
-        block = (bank_own, bank_far)[slot // 2].at[slot % 2, pl.ds(2 * d, 2)]
-        return pltpu.make_async_remote_copy(
-            src_ref=block, dst_ref=block, send_sem=sem,
-            recv_sem=bank_recv.at[slot, d], device_id=(to, me_e), device_id_type=MESH,
+        block = banks[slot // 2].at[slot % 2, pl.ds(2 * d, 2)]
+        return pltpu.make_async_remote_copy(
+            src_ref=block, dst_ref=block, send_sem=bank_send.at[slot // 2],
+            recv_sem=sem, device_id=(to, me_e), device_id_type=MESH,
         )
 
     def first_hop(slot, j):
-        return bank_copy(slot, me_d, along(slot, j), bank_send.at[slot, j - 1])
+        return bank_copy(slot, me_d, along(slot, j), first_recv.at[slot])
 
     def second_hop(slot, b, j):
-        return bank_copy(slot, along(slot, b), along(slot + 1, j), bank_hop.at[slot, b, j - 1])
-
-    def arrival(slot, d):
-        bank_copy(slot, d, along(0, 1), bank_send.at[slot, 0]).wait_recv()
+        return bank_copy(slot, along(slot, b), along(slot + 1, j), second_recv.at[slot // 2])
 
     def open_gather(slots):
         for slot in slots:
@@ -144,20 +153,16 @@
                 second_hop(slot, 0, j).start()
 
     def pass_on(slots):
-        for b in range(1, SIDE):
-            for slot in slots:
-                arrival(slot, along(slot, b))
+        for slot in slots:
+            blocks = banks[slot // 2].at[slot % 2, pl.ds(0, 2 * (SIDE - 1))]
+            batch(blocks, first_recv.at[slot]).wait_recv()
+            for b in range(1, SIDE):
                 for j in range(1, SIDE):
                     second_hop(slot, b, j).start()
 
-    def close_gather(slots):
-        for j in range(1, SIDE):
-            for b in range(SIDE):
-                for slot in slots:
-                    if slot % 2 == 0:
-                        arrival(slot, ((y + j) % SIDE) * SIDE + (x + b) % SIDE)
-                    else:
-                        arrival(slot, ((y + b) % SIDE) * SIDE + (x + j) % SIDE)
+    def close_gather(n):
+        blocks = banks[n].at[:, pl.ds(0, 2 * SIDE * (SIDE - 1))]
+        batch(blocks, second_recv.at[n]).wait_recv()
 
     open_gather((0, 1))
 
@@ -180,40 +185,27 @@
                 keys, v[:, cols], (((0,), (0,)), ((), ())), preferred_element_type=jnp.float32
             ).astype(jnp.bfloat16)
 
-    for cut in range(CUTS):
-        load(0, cut).wait()
-        load(1, cut).wait()
+    loaded(0)
+    loaded(1)
     update(partner(0))
 
     def send_u(e):
         return pltpu.make_async_remote_copy(
-            src_ref=sent_u.at[e], dst_ref=got_u.at[me_e], send_sem=u_send.at[e],
-            recv_sem=u_recv.at[me_e], device_id=(me_d, e), device_id_type=MESH,
-        )
-
-    def recv_u(e):
-        return pltpu.make_async_remote_copy(
-            src_ref=sent_u.at[e], dst_ref=got_u.at[e], send_sem=u_send.at[e],
-            recv_sem=u_recv.at[e], device_id=(me_d, e), device_id_type=MESH,
-        )
-
-    def send_own(e, slot):
-        return pltpu.make_async_remote_copy(
-            src_ref=picked.at[e, slot], dst_ref=got_s.at[me_e, slot], send_sem=s_send.at[e, slot],
-            recv_sem=s_recv.at[me_e, slot], device_id=(me_d, e), device_id_type=MESH,
-        )
-
-    def send_far(e, slot):
+            src_ref=sent_u.at[e], dst_ref=got_u.at[me_e], send_sem=u_sem.at[0],
+            recv_sem=u_sem.at[1], device_id=(me_d, e), device_id_type=MESH,
+        )
+
+    def send_own(e, slot, i):
+        return pltpu.make_async_remote_copy(
+            src_ref=picked.at[e, slot], dst_ref=got_s.at[me_e, slot], send_sem=s_send.at[0],
+            recv_sem=s_recv.at[0, i], device_id=(me_d, e), device_id_type=MESH,
+        )
+
+    def send_far(e, slot, i):
         owner = kept_for(me_e, slot)
         return pltpu.make_async_remote_copy(
-            src_ref=passed.at[e, slot], dst_ref=got_s.at[owner, slot], send_sem=p_send.at[e, slot],
-            recv_sem=s_recv.at[owner, slot], device_id=(me_d, e), device_id_type=MESH,
-        )
-
-    def recv_s(e, slot):
-        return pltpu.make_async_remote_copy(
-            src_ref=picked.at[e, slot], dst_ref=got_s.at[e, slot], send_sem=s_send.at[e, slot],
-            recv_sem=s_recv.at[e, slot], device_id=(me_d, e), device_id_type=MESH,
+            src_ref=passed.at[e, slot], dst_ref=got_s.at[owner, slot], send_sem=s_send.at[1],
+            recv_sem=s_recv.at[1, i], device_id=(me_d, e), device_id_type=MESH,
         )
 
     def update_step(i, _):
@@ -224,16 +216,14 @@
     lax.fori_loop(0, GROUP - 1, update_step, 0)
 
     pass_on((0, 1))
-    swap(0).wait_recv()
-    swap(1).wait_recv()
+    batch(bank_far.at[:, pl.ds(0, 2)], swap_recv.at[0]).wait_recv()
     open_gather((2, 3))
 
     t_of = lax.broadcasted_iota(jnp.int32, (SEG, SEG), 0)
     s_of = lax.broadcasted_iota(jnp.int32, (SEG, SEG), 1)
     offsets[...] = jnp.where(t_of >= s_of, (t_of - s_of).astype(jnp.float32), FAR)
 
-    for cut in range(CUTS):
-        load(2, cut).wait()
+    loaded(2)
 
     def within(i, _):
         cols = pl.ds(pl.multiple_of(i * DIM, DIM), DIM)
@@ -262,13 +252,13 @@
                 step(slot, i)
             return 0
 
-        lax.fori_loop(0, 6, both, 0)
-
-    close_gather((0, 1))
+        lax.fori_loop(0, LAST, both, 0)
+
+    close_gather(0)
     lax.fori_loop(0, GROUP, pick, 0)
-    each_other(lambda slot, i: send_own(taker(slot, i), slot).start())
+    each_other(lambda slot, i: send_own(taker(slot, i), slot, i).start())
     for slot in range(2):
-        send_own(other, slot).start()
+        send_own(other, slot, LAST).start()
 
     lax.fori_loop(MIDDLE, HEADS, within, 0)
 
@@ -283,8 +273,6 @@
 
     def grow_step(i, _):
         e = source(i)
-        recv_u(e).wait_recv()
-        send_u(partner(i)).wait_send()
         grow(e, got_u)
         return 0
 
@@ -294,13 +282,13 @@
     def pass_far(slot, i):
         e = giver(slot, i)
         select(e, slot)
-        send_far(e, slot).start()
-
-    close_gather((2, 3))
+        send_far(e, slot, i).start()
+
+    close_gather(1)
     each_other(pass_far)
     for slot in range(2):
         select(other, slot)
-        send_far(other, slot).start()
+        send_far(other, slot, LAST).start()
         select(me_e, slot)
 
     def finish(owner, slot, src, at):
@@ -309,63 +297,63 @@
         carried = jnp.dot(q[:, cols], src[at, slot], preferred_element_type=jnp.float32)
         att[:, cols] = jnp.where(inside, total[:, cols] + carried * lead, 0.0).astype(jnp.bfloat16)
 
-    def arrived(owner, slot):
-        recv_s(owner, slot).wait_recv()
-        finish(owner, slot, got_s, owner)
-
     def finish_here(slot, _):
         finish(me_e, slot, picked, me_e)
         finish(kept_for(me_e, slot), slot, passed, me_e)
         return 0
 
+    def arrived(kind, i):
+        batch(got_s.at[0], s_recv.at[kind, i]).wait_recv()
+
     def finish_other(slot, _):
-        send_own(other, slot).wait_send()
-        send_far(other, slot).wait_send()
-        arrived(other, slot)
-        arrived(kept_for(other, slot), slot)
-        return 0
-
-    def finish_own(j, _):
-        i, slot = j // 2, j % 2
-        arrived(giver(slot, i), slot)
-        send_own(taker(slot, i), slot).wait_send()
-        return 0
-
-    def finish_far(j, _):
-        i, slot = j // 2, j % 2
-        arrived(kept_for(taker(slot, i), slot), slot)
-        send_far(giver(slot, i), slot).wait_send()
+        for owner in (other, kept_for(other, slot)):
+            finish(owner, slot, got_s, owner)
+        return 0
+
+    def finish_own(i, _):
+        arrived(0, i)
+        for slot in range(2):
+            owner = giver(slot, i)
+            finish(owner, slot, got_s, owner)
+        return 0
+
+    def finish_far(i, _):
+        arrived(1, i)
+        for slot in range(2):
+            owner = kept_for(taker(slot, i), slot)
+            finish(owner, slot, got_s, owner)
         return 0
 
     lax.fori_loop(0, 2, finish_here, 0)
-    swap(0).wait_send()
-    swap(1).wait_send()
-    for slot in range(4):
-        for j in range(1, SIDE):
-            first_hop(slot, j).wait_send()
-            for b in range(SIDE):
-                second_hop(slot, b, j).wait_send()
+    batch(bank_own, bank_send.at[0]).wait_send()
+    batch(bank_far.at[:, pl.ds(0, 2 * SIDE * SIDE - 2)], bank_send.at[1]).wait_send()
+    batch(sent_u.at[pl.ds(0, GROUP - 1)], u_sem.at[0]).wait_send()
+    batch(got_u.at[pl.ds(0, GROUP - 1)], u_sem.at[1]).wait_recv()
     grow(me_e, sent_u)
     lax.fori_loop(0, GROUP - 1, grow_step, 0)
+    for kind in range(2):
+        arrived(kind, LAST)
     lax.fori_loop(0, 2, finish_other, 0)
-    lax.fori_loop(0, 12, finish_own, 0)
-    lax.fori_loop(0, 12, finish_far, 0)
+    lax.fori_loop(0, LAST, finish_own, 0)
+    batch(picked.at[pl.ds(0, LAST + 1)], s_send.at[0]).wait_send()
+    lax.fori_loop(0, LAST, finish_far, 0)
+    batch(passed.at[pl.ds(0, LAST + 1)], s_send.at[1]).wait_send()
 
 
 STEPS = 4
 TOKENS = SEG // STEPS
 
 
-def settle(att, child, gain, mixed_hbm, child_hbm, mixed, child_sem, mixed_sem):
+def settle(att, child, gain, mixed_hbm, child_hbm, mixed, sem):
     kids = GROUP // STEPS
 
     def child_out(at):
         part = pl.ds(at * kids, kids)
-        return pltpu.make_async_copy(child.at[part], child_hbm.at[part], child_sem.at[at])
+        return pltpu.make_async_copy(child.at[part], child_hbm.at[part], sem.at[0])
 
     def mixed_out(at):
         part = pl.ds(at * TOKENS, TOKENS)
-        return pltpu.make_async_copy(mixed.at[part], mixed_hbm.at[part], mixed_sem.at[at])
+        return pltpu.make_async_copy(mixed.at[part], mixed_hbm.at[part], sem.at[1])
 
     def step(at, _):
         here = pl.ds(pl.multiple_of(at * TOKENS, TOKENS), TOKENS)
@@ -378,9 +366,8 @@
     for at in range(STEPS):
         child_out(at).start()
     lax.fori_loop(0, STEPS, step, 0)
-    for at in range(STEPS):
-        child_out(at).wait()
-        mixed_out(at).wait()
+    pltpu.make_async_copy(child, child_hbm, sem.at[0]).wait()
+    pltpu.make_async_copy(mixed, mixed_hbm, sem.at[1]).wait()
 
 
 def body(queries, key_rows, value_rows, slopes, norm_gain, parents, lengths, parent_states):
@@ -419,17 +406,15 @@
             pltpu.VMEM(moved, bf16),
             pltpu.VMEM(moved, bf16),
             pltpu.VMEM(moved, bf16),
-            dma((3, CUTS)),
+            dma((3,)),
             dma((4,)),
-            dma((2, 2)),
-            dma((4, SIDE - 1)),
-            dma((4, SIDE, SIDE - 1)),
-            dma((4, SIDE * SIDE)),
-            dma((GROUP,)),
-            dma((GROUP,)),
-            dma((GROUP, 2)),
-            dma((GROUP, 2)),
-            dma((GROUP, 2)),
+            dma((2,)),
+            dma((1,)),
+            dma((4,)),
+            dma((2,)),
+            dma((2,)),
+            dma((2,)),
+            dma((2, LAST + 1)),
         ],
         compiler_params=pltpu.CompilerParams(
             collective_id=0, has_side_effects=True, vmem_limit_bytes=40 * 1024 * 1024
@@ -446,8 +431,7 @@
         out_specs=(anywhere,) * 2,
         scratch_shapes=[
             pltpu.VMEM((SEG, width), bf16),
-            dma((STEPS,)),
-            dma((STEPS,)),
+            dma((2,)),
         ],
         compiler_params=pltpu.CompilerParams(vmem_limit_bytes=32 * 1024 * 1024),
         name="settle",

time: 54.5 us -> 51.9 us (0.952)
  Pallas kernels: 53.7 us -> 51.2 us
    pallas_call x1, Pallas kernels: 51.7 us -> 49.2 us  [body(): pl.pallas_call(exchange, out_shape=(jax.ShapeDtypeStruct((SEG, width), bf...]
where the time goes in v5:
time: 51.9 us
  Pallas kernels  51.2 us (99%)
  between operations  0.66 us (1%)
    pallas_call x1, Pallas kernels, body(): pl.pallas_call(exchange, out_shape=(jax.ShapeDtypeStruct((SEG, width), bf...  49.2 us
    pallas_call x1, Pallas kernels, body(): pl.pallas_call(settle, out_shape=(jax.ShapeDtypeStruct((SEG, width), bf16...  2.02 us

profile of v5, /device:TPU:1, one launch (start us, length us, event | category | flops | bytes accessed | tf_op | source)
XLA Modules:
  0.0 51.9 jit_solution(14071106587041689714)
XLA Ops:
  0.6 0.0 copy-start
  0.6 49.2 %exchange.1 = (bf16[256,4096]{1,0:T(8,128)(2,1)S(1)}, f32[16,2,128,128]{3,2,1,0:T(8,128)S(1)}) custom-call(bf16[256,4096]{1,0:T(8,128)(2,1)} %q_hbm.1, bf16[256,4096]{1,0:T(8,128)(2,1)} %k_hbm.1, bf16[256,4096]{1,0:T(8,128)(2,1)} %v_hbm.1, f32[32]{0:T(128)} %slopes_hbm.1, s32[16]{0:T(128)} %parents_hbm.1, s32[16]{0:T(128)} %lengths_hbm.1, ...), custom_call_target="tpu_custom_call" | custom-call | tf_op jit(solution)/shard_map/exchange/pallas_call | solution.py:384
  49.8 0.0 copy-done
  49.8 2.0 %settle.1 = (bf16[256,4096]{1,0:T(8,128)(2,1)}, f32[16,2,128,128]{3,2,1,0:T(8,128)}) custom-call(bf16[256,4096]{1,0:T(8,128)(2,1)S(1)} %get-tuple-element.4.att, f32[16,2,128,128]{3,2,1,0:T(8,128)S(1)} %get-tuple-element.5.child, f32[1,4096]{1,0:T(1,128)S(1)} %bitcast.1), custom_call_target="tpu_custom_call" | custom-call | tf_op jit(solution)/shard_map/settle/pallas_call | solution.py:424
Async XLA Ops:
  0.6 49.2 %copy-start = (f32[4096]{0:T(1024)S(1)}, f32[4096]{0:T(1024)}, u32[]{:S(2)}) copy-start(f32[4096]{0:T(1024)} %param.12) | copy-start | bytes 49156

commit v6 on v5

--- a/solution.py
+++ b/solution.py
@@ -53,18 +53,18 @@
 
     barrier = pltpu.get_barrier_semaphore()
 
-    def greet(i, _):
-        pl.semaphore_signal(
-            barrier, inc=1, device_id=(me_d, (me_e + i) % GROUP), device_id_type=MESH
-        )
-        return 0
-
-    lax.fori_loop(1, GROUP, greet, 0)
-    for slot in range(2):
-        for j in range(1, SIDE):
-            pl.semaphore_signal(
-                barrier, inc=1, device_id=(along(slot, j), me_e), device_id_type=MESH
-            )
+    def greet(d, e):
+        pl.semaphore_signal(barrier, inc=1, device_id=(d, e), device_id_type=MESH)
+
+    for i in range(6):
+        off, flip = ring_step(i)
+        greet(me_d, 2 * ((z + off) % RING) + (core + flip) % 2)
+    for j in (2, 1, 3):
+        for slot in range(2):
+            greet(along(slot, j), me_e)
+    for i in range(6, GROUP - 1):
+        off, flip = ring_step(i)
+        greet(me_d, 2 * ((z + off) % RING) + (core + flip) % 2)
 
     smalls = [
         pltpu.make_async_copy(src, dst, small_sem.at[n])
@@ -345,12 +345,6 @@
 
 
 def settle(att, child, gain, mixed_hbm, child_hbm, mixed, sem):
-    kids = GROUP // STEPS
-
-    def child_out(at):
-        part = pl.ds(at * kids, kids)
-        return pltpu.make_async_copy(child.at[part], child_hbm.at[part], sem.at[0])
-
     def mixed_out(at):
         part = pl.ds(at * TOKENS, TOKENS)
         return pltpu.make_async_copy(mixed.at[part], mixed_hbm.at[part], sem.at[1])
@@ -363,10 +357,10 @@
         mixed_out(at).start()
         return 0
 
-    for at in range(STEPS):
-        child_out(at).start()
+    child_out = pltpu.make_async_copy(child, child_hbm, sem.at[0])
+    child_out.start()
     lax.fori_loop(0, STEPS, step, 0)
-    pltpu.make_async_copy(child, child_hbm, sem.at[0]).wait()
+    child_out.wait()
     pltpu.make_async_copy(mixed, mixed_hbm, sem.at[1]).wait()
 
 

time: 51.9 us -> 51.7 us (level)
  no operation moved by 1% of the time
where the time goes in v6:
time: 51.7 us; the launch traced here: 51.6 us
  Pallas kernels  51 us (99%)
  between operations  0.66 us (1%)
    pallas_call x1, Pallas kernels, body(): pl.pallas_call(exchange, out_shape=(jax.ShapeDtypeStruct((SEG, width), bf...  49 us
    pallas_call x1, Pallas kernels, body(): pl.pallas_call(settle, out_shape=(jax.ShapeDtypeStruct((SEG, width), bf16...  2.02 us

profile of v6, /device:TPU:1, one launch (start us, length us, event | category | flops | bytes accessed | tf_op | source)
XLA Modules:
  0.0 51.6 jit_solution(13033486495078089285)
XLA Ops:
  0.6 0.0 copy-start
  0.6 49.0 %exchange.1 = (bf16[256,4096]{1,0:T(8,128)(2,1)S(1)}, f32[16,2,128,128]{3,2,1,0:T(8,128)S(1)}) custom-call(bf16[256,4096]{1,0:T(8,128)(2,1)} %q_hbm.1, bf16[256,4096]{1,0:T(8,128)(2,1)} %k_hbm.1, bf16[256,4096]{1,0:T(8,128)(2,1)} %v_hbm.1, f32[32]{0:T(128)} %slopes_hbm.1, s32[16]{0:T(128)} %parents_hbm.1, s32[16]{0:T(128)} %lengths_hbm.1, ...), custom_call_target="tpu_custom_call" | custom-call | tf_op jit(solution)/shard_map/exchange/pallas_call | solution.py:378
  49.6 0.0 copy-done
  49.6 2.0 %settle.1 = (bf16[256,4096]{1,0:T(8,128)(2,1)}, f32[16,2,128,128]{3,2,1,0:T(8,128)}) custom-call(bf16[256,4096]{1,0:T(8,128)(2,1)S(1)} %get-tuple-element.4.att, f32[16,2,128,128]{3,2,1,0:T(8,128)S(1)} %get-tuple-element.5.child, f32[1,4096]{1,0:T(1,128)S(1)} %bitcast.1), custom_call_target="tpu_custom_call" | custom-call | tf_op jit(solution)/shard_map/settle/pallas_call | solution.py:418
Async XLA Ops:
  0.6 49.0 %copy-start = (f32[4096]{0:T(1024)S(1)}, f32[4096]{0:T(1024)}, u32[]{:S(2)}) copy-start(f32[4096]{0:T(1024)} %param.12) | copy-start | bytes 49156

commit v7 on v6

--- a/solution.py
+++ b/solution.py
@@ -51,6 +51,9 @@
     def along(slot, j):
         return y * SIDE + (x + j) % SIDE if slot % 2 == 0 else ((y + j) % SIDE) * SIDE + x
 
+    def spot(slot, b):
+        return SIDE * (x if slot % 2 else y) + b
+
     barrier = pltpu.get_barrier_semaphore()
 
     def greet(d, e):
@@ -82,7 +85,7 @@
 
     for slot in range(2):
         for parent in range(2):
-            bank_own[slot, 2 * me_d + parent] = states[parent, slot].astype(jnp.bfloat16)
+            bank_own[slot, 2 * spot(slot, 0) + parent] = states[parent, slot].astype(jnp.bfloat16)
 
     def head_columns(e, head):
         return pl.ds(pl.multiple_of(e * PAIR + head * DIM, DIM), DIM)
@@ -114,8 +117,8 @@
 
     def swap(slot):
         return pltpu.make_async_remote_copy(
-            src_ref=bank_own.at[slot, pl.ds(2 * me_d, 2)],
-            dst_ref=bank_far.at[slot, pl.ds(2 * me_d, 2)],
+            src_ref=bank_own.at[slot, pl.ds(2 * spot(slot, 0), 2)],
+            dst_ref=bank_far.at[slot, pl.ds(2 * spot(slot, 0), 2)],
             send_sem=bank_send.at[0], recv_sem=swap_recv.at[0],
             device_id=(me_d, device(SWAP if slot else RING - SWAP, 0)), device_id_type=MESH,
         )
@@ -131,18 +134,20 @@
 
     banks = (bank_own, bank_far)
 
-    def bank_copy(slot, d, to, sem):
-        block = banks[slot // 2].at[slot % 2, pl.ds(2 * d, 2)]
-        return pltpu.make_async_remote_copy(
-            src_ref=block, dst_ref=block, send_sem=bank_send.at[slot // 2],
-            recv_sem=sem, device_id=(to, me_e), device_id_type=MESH,
+    def bank_copy(slot, src, dst, count, to, sem):
+        bank = banks[slot // 2].at[slot % 2]
+        return pltpu.make_async_remote_copy(
+            src_ref=bank.at[pl.ds(2 * src, 2 * count)], dst_ref=bank.at[pl.ds(2 * dst, 2 * count)],
+            send_sem=bank_send.at[slot // 2], recv_sem=sem, device_id=(to, me_e), device_id_type=MESH,
         )
 
     def first_hop(slot, j):
-        return bank_copy(slot, me_d, along(slot, j), first_recv.at[slot])
-
-    def second_hop(slot, b, j):
-        return bank_copy(slot, along(slot, b), along(slot + 1, j), second_recv.at[slot // 2])
+        to = along(slot, j)
+        return bank_copy(slot, spot(slot, 0), spot(slot, SIDE - j), 1, to, first_recv.at[slot])
+
+    def second_hop(slot, b, count, j):
+        at, to = spot(slot, b), along(slot + 1, j)
+        return bank_copy(slot, at, at, count, to, second_recv.at[slot // 2])
 
     def open_gather(slots):
         for slot in slots:
@@ -150,15 +155,14 @@
                 first_hop(slot, j).start()
         for slot in slots:
             for j in range(1, SIDE):
-                second_hop(slot, 0, j).start()
+                second_hop(slot, 0, 1, j).start()
 
     def pass_on(slots):
         for slot in slots:
             blocks = banks[slot // 2].at[slot % 2, pl.ds(0, 2 * (SIDE - 1))]
             batch(blocks, first_recv.at[slot]).wait_recv()
-            for b in range(1, SIDE):
-                for j in range(1, SIDE):
-                    second_hop(slot, b, j).start()
+            for j in range(1, SIDE):
+                second_hop(slot, 1, SIDE - 1, j).start()
 
     def close_gather(n):
         blocks = banks[n].at[:, pl.ds(0, 2 * SIDE * (SIDE - 1))]
@@ -240,10 +244,16 @@
     pass_on((2, 3))
     lax.fori_loop(EARLY, MIDDLE, within, 0)
 
+    def held(e, slot):
+        parent = parents[e]
+        half, mine = parent % 2, parent // 2
+        down, right = mine // SIDE, mine % SIDE
+        row, step = (right, down - y) if slot else (down, right - x)
+        return 2 * (SIDE * row + (step + SIDE) % SIDE) + half
+
     def pick(e, _):
-        parent = parents[e]
         for slot in range(2):
-            picked[e, slot] = bank_own[slot, parent]
+            picked[e, slot] = bank_own[slot, held(e, slot)]
         return 0
 
     def each_other(step):
@@ -277,7 +287,7 @@
         return 0
 
     def select(e, slot):
-        passed[e, slot] = bank_far[slot, parents[e]]
+        passed[e, slot] = bank_far[slot, held(e, slot)]
 
     def pass_far(slot, i):
         e = giver(slot, i)

time: 51.7 us -> 51.9 us (level)
  no operation moved by 1% of the time
where the time goes in v7:
time: 51.9 us; the launch traced here: 51.8 us
  Pallas kernels  51.2 us (99%)
  between operations  0.66 us (1%)
    pallas_call x1, Pallas kernels, body(): pl.pallas_call(exchange, out_shape=(jax.ShapeDtypeStruct((SEG, width), bf...  49.2 us
    pallas_call x1, Pallas kernels, body(): pl.pallas_call(settle, out_shape=(jax.ShapeDtypeStruct((SEG, width), bf16...  2.02 us

profile of v7, /device:TPU:1, one launch (start us, length us, event | category | flops | bytes accessed | tf_op | source)
XLA Modules:
  0.0 51.8 jit_solution(18206489756246769222)
XLA Ops:
  0.6 0.0 copy-start
  0.6 49.2 %exchange.1 = (bf16[256,4096]{1,0:T(8,128)(2,1)S(1)}, f32[16,2,128,128]{3,2,1,0:T(8,128)S(1)}) custom-call(bf16[256,4096]{1,0:T(8,128)(2,1)} %q_hbm.1, bf16[256,4096]{1,0:T(8,128)(2,1)} %k_hbm.1, bf16[256,4096]{1,0:T(8,128)(2,1)} %v_hbm.1, f32[32]{0:T(128)} %slopes_hbm.1, s32[16]{0:T(128)} %parents_hbm.1, s32[16]{0:T(128)} %lengths_hbm.1, ...), custom_call_target="tpu_custom_call" | custom-call | tf_op jit(solution)/shard_map/exchange/pallas_call | solution.py:388
  49.8 0.0 copy-done
  49.8 2.0 %settle.1 = (bf16[256,4096]{1,0:T(8,128)(2,1)}, f32[16,2,128,128]{3,2,1,0:T(8,128)}) custom-call(bf16[256,4096]{1,0:T(8,128)(2,1)S(1)} %get-tuple-element.4.att, f32[16,2,128,128]{3,2,1,0:T(8,128)S(1)} %get-tuple-element.5.child, f32[1,4096]{1,0:T(1,128)S(1)} %bitcast.1), custom_call_target="tpu_custom_call" | custom-call | tf_op jit(solution)/shard_map/settle/pallas_call | solution.py:428
Async XLA Ops:
  0.6 49.2 %copy-start = (f32[4096]{0:T(1024)S(1)}, f32[4096]{0:T(1024)}, u32[]{:S(2)}) copy-start(f32[4096]{0:T(1024)} %param.12) | copy-start | bytes 49156

commit v8 on v5

--- a/solution.py
+++ b/solution.py
@@ -187,7 +187,7 @@
 
     loaded(0)
     loaded(1)
-    update(partner(0))
+    update(partner(GROUP - 3))
 
     def send_u(e):
         return pltpu.make_async_remote_copy(
@@ -209,11 +209,13 @@
         )
 
     def update_step(i, _):
-        send_u(partner(i)).start()
-        update(partner(i + 1))
-        return 0
-
-    lax.fori_loop(0, GROUP - 1, update_step, 0)
+        send_u(partner(GROUP - 3 - i)).start()
+        update(partner((2 * GROUP - 4 - i) % GROUP))
+        return 0
+
+    lax.fori_loop(0, GROUP - 2, update_step, 0)
+    update(other)
+    send_u(other).start()
 
     pass_on((0, 1))
     batch(bank_far.at[:, pl.ds(0, 2)], swap_recv.at[0]).wait_recv()

time: 51.9 us -> 52.5 us (1.012)
    pallas_call x1, Pallas kernels: 49.2 us -> 49.7 us  [body(): pl.pallas_call(exchange, out_shape=(jax.ShapeDtypeStruct((SEG, width), bf...]
where the time goes in v8:
time: 52.5 us; the launch traced here: 52.4 us
  Pallas kernels  51.7 us (98%)
  between operations  0.66 us (1%)
    pallas_call x1, Pallas kernels, body(): pl.pallas_call(exchange, out_shape=(jax.ShapeDtypeStruct((SEG, width), bf...  49.7 us
    pallas_call x1, Pallas kernels, body(): pl.pallas_call(settle, out_shape=(jax.ShapeDtypeStruct((SEG, width), bf16...  2.02 us

profile of v8, /device:TPU:1, one launch (start us, length us, event | category | flops | bytes accessed | tf_op | source)
XLA Modules:
  0.0 52.4 jit_solution(6731146527089760253)
XLA Ops:
  0.6 0.0 copy-start
  0.6 49.7 %exchange.1 = (bf16[256,4096]{1,0:T(8,128)(2,1)S(1)}, f32[16,2,128,128]{3,2,1,0:T(8,128)S(1)}) custom-call(bf16[256,4096]{1,0:T(8,128)(2,1)} %q_hbm.1, bf16[256,4096]{1,0:T(8,128)(2,1)} %k_hbm.1, bf16[256,4096]{1,0:T(8,128)(2,1)} %v_hbm.1, f32[32]{0:T(128)} %slopes_hbm.1, s32[16]{0:T(128)} %parents_hbm.1, s32[16]{0:T(128)} %lengths_hbm.1, ...), custom_call_target="tpu_custom_call" | custom-call | tf_op jit(solution)/shard_map/exchange/pallas_call | solution.py:386
  50.4 0.0 copy-done
  50.4 2.0 %settle.1 = (bf16[256,4096]{1,0:T(8,128)(2,1)}, f32[16,2,128,128]{3,2,1,0:T(8,128)}) custom-call(bf16[256,4096]{1,0:T(8,128)(2,1)S(1)} %get-tuple-element.4.att, f32[16,2,128,128]{3,2,1,0:T(8,128)S(1)} %get-tuple-element.5.child, f32[1,4096]{1,0:T(1,128)S(1)} %bitcast.1), custom_call_target="tpu_custom_call" | custom-call | tf_op jit(solution)/shard_map/settle/pallas_call | solution.py:426
Async XLA Ops:
  0.6 49.7 %copy-start = (f32[4096]{0:T(1024)S(1)}, f32[4096]{0:T(1024)}, u32[]{:S(2)}) copy-start(f32[4096]{0:T(1024)} %param.12) | copy-start | bytes 49156
